TPU v7x, 32 devices: a whole 2x2x4 slice. The times are simulated.
32 devices in a mesh: group: 2 (over x), space: 16 (over z, y, core).
Axes of the slice: x: 2, y: 2, z: 4, core: 2. Of those that a mesh axis runs over, the one named last changes fastest.
Arguments:
- source: float32 [128, 32768], P('space', 'group'), parts along dimension 1, may hold values from -6 to 6
- blocks: float32 [512, 64, 448], P(('group', 'space')), parts along dimension 0, as said below
- columns: int32 [512, 7], P(('group', 'space')), parts along dimension 0, may hold values from 0 to 23, as said below
- rows_up: int32 [128], P(('group', 'space')), parts along dimension 0, may hold values from 0 to 15, as said below
- rows_down: int32 [128], P(('group', 'space')), parts along dimension 0, may hold values from 0 to 15, as said below
Outputs:
- field: float32 [128, 32768], P('space', 'group'), parts along dimension 1
There are 2 independent parts, one for each index of `group`. A program takes and returns all parts, laid end to end along the dimension named above; each array names one. Nothing has to cross between parts.
Inputs may be any that keep to these rules, and one draw needn't show every extreme that they name: `columns`: entry 0 of each row is the row itself, entry 1 a column from 16 to 19, entry 2 one from 20 on, entries 3 to 6 below 16; every received row is named by some row of its device. `rows_up`: 4 distinct row numbers of each device; device 0's include row 0 and row 15. `rows_down`: 4 distinct row numbers of each device; device 1's include row 0 and row 15. `blocks`: slot 0 holds a diagonal of 3 to 5 plus small entries; all other entries are small.
All inputs are finite; a program needn't handle non-finite values.
Results may differ from a plain program's by a relative error of at most 0.0003.
Values sent between devices are 32-bit elements; how exact they have to be, the bound alone decides.
No kernel may reach another device: no remote copies, remote signals or barrier semaphores. Data moves between devices by JAX's collectives and lax.ppermute only.
A program may use at most 64 MiB of HBM per device.

v0:
```python
import jax
import jax.numpy as jnp
from jax import lax
from jax.sharding import PartitionSpec as P

BS = 64
SLOTS = 7
L = 128


shift_scale = 2.0
diag_center = 4.0


def from_behind(value, axis, steps):
    count = lax.axis_size(axis)
    leading, last = (max(0, -steps), min(count, count - steps))
    return lax.ppermute(value, axis, [(source, source + steps) for source in range(leading, last)])


def angles():
    steps = jnp.arange(L, dtype=jnp.int32)
    phase = steps[:, None] * steps[None, :] % L
    return phase.astype(jnp.float32) * (2.0 * jnp.pi / L)


def factors(count):
    freq = jnp.arange(count, dtype=jnp.int32).astype(jnp.float32) * (2.0 * jnp.pi / L)
    shift_re = shift_scale * (1.0 - jnp.cos(freq))
    shift_im = shift_scale * jnp.sin(freq)
    denom = (diag_center + shift_re) ** 2 + shift_im**2
    return (shift_re, shift_im, (diag_center + shift_re) / denom, -shift_im / denom)


def full_mul(factor_re, factor_im, values):
    val_re = values[..., :L]
    val_im = values[..., L:]
    return jnp.concatenate(
        [factor_re * val_re - factor_im * val_im, factor_re * val_im + factor_im * val_re], axis=-1
    )


def per_device(source, blocks, columns, rows_up, rows_down):
    hp = lax.Precision.HIGHEST
    br_local = blocks.shape[0]
    local = lax.all_to_all(source, "space", split_axis=1, concat_axis=0, tiled=True)
    table = angles()
    cosines = jnp.cos(table)
    sines = jnp.sin(table)
    forward = jnp.concatenate([cosines, -sines], axis=1)
    inverse = jnp.concatenate([cosines, -sines], axis=1) / L
    shift_re, shift_im, step_re, step_im = factors(L)
    width = forward.shape[1]
    spectrum = jnp.einsum("tn,tc->nc", local, forward, precision=hp).reshape(br_local, BS, width)
    iterate = full_mul(step_re, step_im, spectrum)
    for sweep in range(3):
        send_down = iterate[rows_down]
        send_up = iterate[rows_up]
        below = from_behind(send_up, "space", 1)
        above = from_behind(send_down, "space", -1)
        widened = jnp.concatenate([iterate, below, above], axis=0)
        gathered = widened[columns].reshape(br_local, SLOTS * BS, width)
        applied = jnp.einsum("rak,rkc->rac", blocks, gathered, precision=hp)
        iterate = iterate + full_mul(
            step_re, step_im, spectrum - (applied + full_mul(shift_re, shift_im, iterate))
        )
    timed = jnp.einsum("nc,tc->tn", iterate.reshape(br_local * BS, width), inverse, precision=hp)
    return lax.all_to_all(timed, "space", split_axis=0, concat_axis=1, tiled=True)


def solution(mesh):
    placed = (
        P("space", "group"),
        P(("group", "space"), None, None),
        P(("group", "space"), None),
        P(("group", "space")),
        P(("group", "space")),
    )
    return jax.shard_map(
        per_device, mesh=mesh, in_specs=placed, out_specs=P("space", "group"), check_vma=False
    )
```

profile of v0, /device:TPU:0, one launch (start us, length us, event | category | flops | bytes accessed | tf_op | source)
XLA Modules:
  0.0 149.2 jit_solution(14796971604824582996)
XLA Ops:
  0.0 7.5 %all-to-all-start = ((f32[8,16,1024]{2,0,1:T(8,128)}), f32[8,16,1024]{2,0,1:T(8,128)S(1)}, u32[]{:S(2)}, u32[]{:S(2)}) async-start(f32[8,16,1024]{2,0,1:T(8,128)} %bitcast.66), calls=%async_computation | async-start | bytes 1048576 | tf_op jit(solution)/shard_map/all_to_all | solution.py:46
  7.6 0.7 compare_select_fusion.2
  8.3 0.7 compare_select_fusion
  9.2 0.7 compare_select_fusion.1
  9.8 0.6 pad_clamp_fusion.1
  10.4 0.3 sine_negate_fusion
  10.7 0.3 fusion.42
  11.1 10.9 %all-to-all-done = f32[8,16,1024]{2,0,1:T(8,128)S(1)} async-done(((f32[8,16,1024]{2,0,1:T(8,128)}), f32[8,16,1024]{2,0,1:T(8,128)S(1)}, u32[]{:S(2)}, u32[]{:S(2)}) %all-to-all-start) | async-done | bytes 524320 | tf_op jit(solution)/shard_map/all_to_all | solution.py:46
  22.0 2.0 %convolution_bitcast_fusion.3 = f32[1024,256]{0,1:T(8,128)} fusion(f32[8,16,1024]{2,0,1:T(8,128)S(1)} %all-to-all-done, f32[128,128]{1,0:T(8,128)S(1)} %get-tuple-element.20, f32[128,128]{1,0:T(8,128)S(1)} %get-tuple-element.21), kind=kOutput, calls=%fused_computation.15 | convolution fusion | flops 402685952 | bytes 1703936 | tf_op jit(solution)/shard_map/tn,tc->nc/dot_general | solution.py:54
  24.0 1.6 %copy.12 = f32[1024,256]{1,0:T(8,128)S(1)} copy(f32[1024,256]{0,1:T(8,128)} %convolution_bitcast_fusion.3) | data formatting | bytes 2097152 | tf_op jit(solution)/shard_map/tn,tc->nc/dot_general | solution.py:54
  25.6 1.0 multiply_subtract_fusion.5
  26.6 0.8 copy-done.3
  27.6 1.1 pad_maximum_fusion.3
  28.6 2.5 %gather_fusion = f32[4,64,256]{2,1,0:T(8,128)} fusion(f32[16,64,256]{2,1,0:T(8,128)} %pad_maximum_fusion.3, s32[1024]{0:T(1024)S(1)} %pad_clamp_fusion.2), kind=kCustom, calls=%fused_computation | custom fusion | bytes 524304 | tf_op jit(solution)/shard_map/gather | solution.py:58
  31.1 1.9 %collective-permute-start = (f32[4,64,256]{2,1,0:T(8,128)}, f32[4,64,256]{2,1,0:T(8,128)S(1)}, u32[]{:S(2)}, u32[]{:S(2)}) collective-permute-start(f32[4,64,256]{2,1,0:T(8,128)} %gather_fusion), channel_id=1, source_target_pairs={{0,1},{1,2},{2,3},{3,4},{4,5},{5,6},{6,7},{7,8},{8,9},{9,10},{10,1... | collective-permute-start | bytes 786440 | tf_op jit(solution)/shard_map/ppermute | solution.py:18
  33.1 2.6 %gather_fusion.1 = f32[4,64,256]{2,1,0:T(8,128)} fusion(f32[16,64,256]{2,1,0:T(8,128)} %pad_maximum_fusion.3, s32[1024]{0:T(1024)} %pad_clamp_fusion.1), kind=kCustom, calls=%fused_computation.1 | custom fusion | bytes 524304 | tf_op jit(solution)/shard_map/gather | solution.py:57
  35.7 1.3 collective-permute-start.1
  37.0 2.1 %multiply_add_fusion.5 = f32[16,64,128]{2,1,0:T(8,128)} fusion(f32[16,64,128]{2,1,0:T(8,128)} %copy-done.3, f32[16,64,128]{2,1,0:T(8,128)} %copy-done.6, f32[128]{0:T(128)S(1)} %get-tuple-element.24, f32[128]{0:T(128)S(1)} %get-tuple-element.25), kind=kLoop, calls=%fused_computation.52 | loop fusion | flops 393216 | bytes 1573888 | tf_op jit(solution)/shard_map/add | solution.py:39
  39.1 0.3 collective-permute-done.1
  39.3 2.6 %pad_maximum_fusion = f32[24,64,256]{2,1,0:T(8,128)} fusion(f32[4,64,256]{2,1,0:T(8,128)S(1)} %collective-permute-done.1, f32[4,64,256]{2,1,0:T(8,128)S(1)} %collective-permute-done, f32[16,64,128]{2,1,0:T(8,128)} %copy-done.6, f32[16,64,128]{2,1,0:T(8,128)} %copy-done.3), kind=kLoop, calls=%fused_computation.9 | loop fusion | flops 1179648 | bytes 3145728 | tf_op jit(solution)/shard_map/concatenate | solution.py:61
  41.9 5.3 %gather_fusion.2 = f32[112,64,256]{2,1,0:T(8,128)} fusion(f32[24,64,256]{2,1,0:T(8,128)} %pad_maximum_fusion, s32[1024]{0:T(1024)S(1)} %pad_clamp_fusion), kind=kCustom, calls=%fused_computation.2 | custom fusion | bytes 14680512 | tf_op jit(solution)/shard_map/gather | solution.py:62
  47.2 8.3 %fusion.1 = f32[16,64,256]{2,1,0:T(8,128)S(1)} fusion(f32[16,64,256]{2,1,0:T(8,128)S(1)} %bitcast.54, f32[16,448,256]{2,1,0:T(8,128)} %bitcast.51, f32[16,64,448]{2,1,0:T(8,128)S(1)} %copy-done, f32[16,64,128]{2,1,0:T(8,128)} %multiply_add_fusion.5, f32[16,64,128]{2,1,0:T(8,128)} %get-tuple-element.5), kind=kOutput, calls=%fused_computation.17 | convolution fusion | flops 1410072576 | bytes 12320768 | tf_op jit(solution)/shard_map/rak,rkc->rac/dot_general | solution.py:63
  55.7 0.8 copy-done.10
  56.7 0.4 copy-done.7
  57.0 1.1 maximum_add_fusion.1
  58.1 2.6 %gather_fusion.3 = f32[4,64,256]{2,1,0:T(8,128)} fusion(f32[16,64,256]{2,1,0:T(8,128)} %maximum_add_fusion.1, s32[1024]{0:T(1024)} %copy-done.22), kind=kCustom, calls=%fused_computation.3 | custom fusion | bytes 524304 | tf_op jit(solution)/shard_map/gather | solution.py:58
  60.8 1.9 %gather_fusion.4 = f32[4,64,256]{2,1,0:T(8,128)S(1)} fusion(f32[16,64,256]{2,1,0:T(8,128)} %maximum_add_fusion.1, s32[1024]{0:T(1024)} %pad_clamp_fusion.1), kind=kCustom, calls=%fused_computation.4 | custom fusion | bytes 524304 | tf_op jit(solution)/shard_map/gather | solution.py:57
  62.7 6.8 %collective-permute-start.2 = (f32[4,64,256]{2,1,0:T(8,128)}, f32[4,64,256]{2,1,0:T(8,128)S(1)}, u32[]{:S(2)}, u32[]{:S(2)}) collective-permute-start(f32[4,64,256]{2,1,0:T(8,128)} %gather_fusion.3), channel_id=1, source_target_pairs={{0,1},{1,2},{2,3},{3,4},{4,5},{5,6},{6,7},{7,8},{8,9},{9,10},{10,1... | collective-permute-start | bytes 786440 | tf_op jit(solution)/shard_map/ppermute | solution.py:18
  69.5 1.5 collective-permute-start.3
  71.0 2.4 %multiply_subtract_fusion.3 = (f32[16,64,128]{2,1,0:T(8,128)}, f32[16,64,128]{2,1,0:T(8,128)}) fusion(f32[16,64,256]{2,1,0:T(8,128)} %maximum_add_fusion.1, f32[128]{0:T(128)S(1)} %get-tuple-element.24, f32[128]{0:T(128)S(1)} %get-tuple-element.25), kind=kLoop, calls=%fused_computation.49 | loop fusion | flops 786432 | bytes 2098176 | tf_op jit(solution)/shard_map/sub | solution.py:39
  73.4 1.4 pad_maximum_fusion.1
  74.8 5.3 %gather_fusion.5 = f32[112,64,256]{2,1,0:T(8,128)} fusion(f32[24,64,256]{2,1,0:T(8,128)} %pad_maximum_fusion.1, s32[1024]{0:T(1024)S(1)} %pad_clamp_fusion), kind=kCustom, calls=%fused_computation.5 | custom fusion | bytes 14680512 | tf_op jit(solution)/shard_map/gather | solution.py:62
  80.1 8.3 %fusion.3 = f32[16,64,256]{2,1,0:T(8,128)S(1)} fusion(f32[16,64,256]{2,1,0:T(8,128)S(1)} %bitcast.55, f32[16,448,256]{2,1,0:T(8,128)} %bitcast.52, f32[16,64,448]{2,1,0:T(8,128)S(1)} %copy-done, f32[16,64,128]{2,1,0:T(8,128)} %get-tuple-element.15, f32[16,64,128]{2,1,0:T(8,128)} %get-tuple-element.14), kind=kOutput, calls=%fused_computation.19 | convolution fusion | flops 1410072576 | bytes 12320768 | tf_op jit(solution)/shard_map/rak,rkc->rac/dot_general | solution.py:63
  88.6 0.8 copy-done.14
  89.6 0.4 copy-done.2
  90.0 1.1 maximum_add_fusion.2
  91.1 2.6 %gather_fusion.6 = f32[4,64,256]{2,1,0:T(8,128)} fusion(f32[16,64,256]{2,1,0:T(8,128)} %maximum_add_fusion.2, s32[1024]{0:T(1024)} %copy-done.22), kind=kCustom, calls=%fused_computation.6 | custom fusion | bytes 524304 | tf_op jit(solution)/shard_map/gather | solution.py:58
  93.7 1.9 %gather_fusion.7 = f32[4,64,256]{2,1,0:T(8,128)S(1)} fusion(f32[16,64,256]{2,1,0:T(8,128)} %maximum_add_fusion.2, s32[1024]{0:T(1024)} %pad_clamp_fusion.1), kind=kCustom, calls=%fused_computation.7 | custom fusion | bytes 524304 | tf_op jit(solution)/shard_map/gather | solution.py:57
  95.6 7.3 %collective-permute-start.4 = (f32[4,64,256]{2,1,0:T(8,128)}, f32[4,64,256]{2,1,0:T(8,128)S(1)}, u32[]{:S(2)}, u32[]{:S(2)}) collective-permute-start(f32[4,64,256]{2,1,0:T(8,128)} %gather_fusion.6), channel_id=1, source_target_pairs={{0,1},{1,2},{2,3},{3,4},{4,5},{5,6},{6,7},{7,8},{8,9},{9,10},{10,1... | collective-permute-start | bytes 786440 | tf_op jit(solution)/shard_map/ppermute | solution.py:18
  102.9 1.3 collective-permute-start.5
  104.2 2.3 %multiply_subtract_fusion.1 = (f32[16,64,128]{2,1,0:T(8,128)}, f32[16,64,128]{2,1,0:T(8,128)}) fusion(f32[16,64,256]{2,1,0:T(8,128)} %maximum_add_fusion.2, f32[128]{0:T(128)S(1)} %get-tuple-element.24, f32[128]{0:T(128)S(1)} %get-tuple-element.25), kind=kLoop, calls=%fused_computation.45 | loop fusion | flops 786432 | bytes 2098176 | tf_op jit(solution)/shard_map/sub | solution.py:39
  106.6 1.4 pad_maximum_fusion.2
  108.0 5.3 %gather_fusion.8 = f32[112,64,256]{2,1,0:T(8,128)} fusion(f32[24,64,256]{2,1,0:T(8,128)} %pad_maximum_fusion.2, s32[1024]{0:T(1024)S(1)} %pad_clamp_fusion), kind=kCustom, calls=%fused_computation.8 | custom fusion | bytes 14680512 | tf_op jit(solution)/shard_map/gather | solution.py:62
  113.3 8.4 %fusion.5 = f32[16,64,256]{2,1,0:T(8,128)S(1)} fusion(f32[16,64,256]{2,1,0:T(8,128)S(1)} %bitcast.56, f32[16,448,256]{2,1,0:T(8,128)} %bitcast.50, f32[16,64,448]{2,1,0:T(8,128)S(1)} %copy-done, f32[16,64,128]{2,1,0:T(8,128)} %get-tuple-element.11, f32[16,64,128]{2,1,0:T(8,128)} %get-tuple-element.10), kind=kOutput, calls=%fused_computation.21 | convolution fusion | flops 1410072576 | bytes 12320768 | tf_op jit(solution)/shard_map/rak,rkc->rac/dot_general | solution.py:63
  121.9 0.8 copy-done.5
  123.2 1.2 fusion.9
  124.5 23.9 %all_to_all.35 = f32[16,8,1024]{2,1,0:T(8,128)S(1)} all-to-all(f32[16,8,1024]{2,1,0:T(8,128)S(1)} %fusion.9), channel_id=1, replica_groups=mesh['group'=2,'space'=16] {'space'}, dimensions={0} | all-to-all | bytes 1048576 | tf_op jit(solution)/shard_map/all_to_all | solution.py:68
  148.4 0.8 copy.15
  (55 shorter events, 1.9 us)
Async XLA Ops:
  0.0 47.2 %copy-start = (f32[16,64,448]{2,1,0:T(8,128)S(1)}, f32[16,64,448]{2,1,0:T(8,128)}, u32[]{:S(2)}) copy-start(f32[16,64,448]{2,1,0:T(8,128)} %param.6) | copy-start | bytes 5505028
  0.0 22.0 %all-to-all-start = ((f32[8,16,1024]{2,0,1:T(8,128)}), f32[8,16,1024]{2,0,1:T(8,128)S(1)}, u32[]{:S(2)}, u32[]{:S(2)}) async-start(f32[8,16,1024]{2,0,1:T(8,128)} %bitcast.66), calls=%async_computation | async-start | bytes 1048576 | tf_op jit(solution)/shard_map/all_to_all | solution.py:46
  7.6 19.0 %copy-start.18 = (f32[128]{0:T(128)}, f32[128]{0:T(128)S(1)}, u32[]{:S(2)}) copy-start(f32[128]{0:T(128)S(1)} %get-tuple-element.23) | copy-start | bytes 1540
  8.3 20.4 %copy-start.22 = (s32[1024]{0:T(1024)}, s32[1024]{0:T(1024)S(1)}, u32[]{:S(2)}) copy-start(s32[1024]{0:T(1024)S(1)} %pad_clamp_fusion.2) | copy-start | bytes 12292
  26.6 0.8 copy-start.3
  26.6 1.0 copy-start.6
  31.1 7.9 %collective-permute-start = (f32[4,64,256]{2,1,0:T(8,128)}, f32[4,64,256]{2,1,0:T(8,128)S(1)}, u32[]{:S(2)}, u32[]{:S(2)}) collective-permute-start(f32[4,64,256]{2,1,0:T(8,128)} %gather_fusion), channel_id=1, source_target_pairs={{0,1},{1,2},{2,3},{3,4},{4,5},{5,6},{6,7},{7,8},{8,9},{9,10},{10,1... | collective-permute-start | bytes 786440 | tf_op jit(solution)/shard_map/ppermute | solution.py:18
  35.7 3.6 %collective-permute-start.1 = (f32[4,64,256]{2,1,0:T(8,128)}, f32[4,64,256]{2,1,0:T(8,128)S(1)}, u32[]{:S(2)}, u32[]{:S(2)}) collective-permute-start(f32[4,64,256]{2,1,0:T(8,128)} %gather_fusion.1), channel_id=1, source_target_pairs={{1,0},{2,1},{3,2},{4,3},{5,4},{6,5},{7,6},{8,7},{9,8},{10,9},{11,1... | collective-permute-start | bytes 786440 | tf_op jit(solution)/shard_map/ppermute | solution.py:18
  47.2 8.3 %copy-start.19 = (f32[128]{0:T(128)S(1)}, f32[128]{0:T(128)}, u32[]{:S(2)}) copy-start(f32[128]{0:T(128)} %copy-done.18) | copy-start | bytes 1540
  55.5 1.1 copy-start.4
  55.5 1.5 %copy-start.7 = (f32[16,64,128]{2,1,0:T(8,128)S(1)}, f32[16,64,128]{2,1,0:T(8,128)}, u32[]{:S(2)}) copy-start(f32[16,64,128]{2,1,0:T(8,128)} %copy-done.6) | copy-start | bytes 1572868
  55.7 0.8 copy-start.10
  55.7 1.0 copy-start.12
  62.7 10.7 %copy-start.1 = (f32[16,64,256]{2,1,0:T(8,128)S(1)}, f32[16,64,256]{2,1,0:T(8,128)}, u32[]{:S(2)}) copy-start(f32[16,64,256]{2,1,0:T(8,128)} %maximum_add_fusion.1) | copy-start | bytes 3145732
  62.7 10.7 %collective-permute-start.2 = (f32[4,64,256]{2,1,0:T(8,128)}, f32[4,64,256]{2,1,0:T(8,128)S(1)}, u32[]{:S(2)}, u32[]{:S(2)}) collective-permute-start(f32[4,64,256]{2,1,0:T(8,128)} %gather_fusion.3), channel_id=1, source_target_pairs={{0,1},{1,2},{2,3},{3,4},{4,5},{5,6},{6,7},{7,8},{8,9},{9,10},{10,1... | collective-permute-start | bytes 786440 | tf_op jit(solution)/shard_map/ppermute | solution.py:18
  69.5 3.9 %collective-permute-start.3 = (f32[4,64,256]{2,1,0:T(8,128)S(1)}, f32[4,64,256]{2,1,0:T(8,128)S(1)}, u32[]{:S(2)}, u32[]{:S(2)}) collective-permute-start(f32[4,64,256]{2,1,0:T(8,128)S(1)} %gather_fusion.4), channel_id=1, source_target_pairs={{1,0},{2,1},{3,2},{4,3},{5,4},{6,5},{7,6},{8,7},{9,8},{10,9},{11,1... | collective-permute-start | bytes 786440 | tf_op jit(solution)/shard_map/ppermute | solution.py:18
  80.1 8.3 %copy-start.20 = (f32[128]{0:T(128)S(1)}, f32[128]{0:T(128)}, u32[]{:S(2)}) copy-start(f32[128]{0:T(128)} %copy-done.18) | copy-start | bytes 1540
  88.4 1.6 %copy-start.2 = (f32[16,64,256]{2,1,0:T(8,128)S(1)}, f32[16,64,256]{2,1,0:T(8,128)}, u32[]{:S(2)}) copy-start(f32[16,64,256]{2,1,0:T(8,128)} %maximum_add_fusion.1) | copy-start | bytes 3145732
  88.6 0.8 copy-start.14
  88.6 1.0 copy-start.16
  95.6 10.9 %copy-start.9 = (f32[16,64,256]{2,1,0:T(8,128)S(1)}, f32[16,64,256]{2,1,0:T(8,128)}, u32[]{:S(2)}) copy-start(f32[16,64,256]{2,1,0:T(8,128)} %maximum_add_fusion.2) | copy-start | bytes 3145732
  95.6 10.9 %collective-permute-start.4 = (f32[4,64,256]{2,1,0:T(8,128)}, f32[4,64,256]{2,1,0:T(8,128)S(1)}, u32[]{:S(2)}, u32[]{:S(2)}) collective-permute-start(f32[4,64,256]{2,1,0:T(8,128)} %gather_fusion.6), channel_id=1, source_target_pairs={{0,1},{1,2},{2,3},{3,4},{4,5},{5,6},{6,7},{7,8},{8,9},{9,10},{10,1... | collective-permute-start | bytes 786440 | tf_op jit(solution)/shard_map/ppermute | solution.py:18
  102.9 3.6 %collective-permute-start.5 = (f32[4,64,256]{2,1,0:T(8,128)S(1)}, f32[4,64,256]{2,1,0:T(8,128)S(1)}, u32[]{:S(2)}, u32[]{:S(2)}) collective-permute-start(f32[4,64,256]{2,1,0:T(8,128)S(1)} %gather_fusion.7), channel_id=1, source_target_pairs={{1,0},{2,1},{3,2},{4,3},{5,4},{6,5},{7,6},{8,7},{9,8},{10,9},{11,1... | collective-permute-start | bytes 786440 | tf_op jit(solution)/shard_map/ppermute | solution.py:18
  113.3 8.4 %copy-start.21 = (f32[128]{0:T(128)S(1)}, f32[128]{0:T(128)}, u32[]{:S(2)}) copy-start(f32[128]{0:T(128)} %copy-done.18) | copy-start | bytes 1540
  113.3 8.6 %copy-start.15 = (f32[16,64,128]{2,1,0:T(8,128)S(1)}, f32[16,64,128]{2,1,0:T(8,128)}, u32[]{:S(2)}) copy-start(f32[16,64,128]{2,1,0:T(8,128)} %copy-done.14) | copy-start | bytes 1572868
  113.3 8.6 %copy-start.17 = (f32[16,64,128]{2,1,0:T(8,128)S(1)}, f32[16,64,128]{2,1,0:T(8,128)}, u32[]{:S(2)}) copy-start(f32[16,64,128]{2,1,0:T(8,128)} %copy-done.16) | copy-start | bytes 1572868
  121.7 1.0 copy-start.5
  121.7 1.2 copy-start.8
  121.7 1.3 copy-start.11
  121.8 1.5 %copy-start.13 = (f32[16,64,128]{2,1,0:T(8,128)S(1)}, f32[16,64,128]{2,1,0:T(8,128)}, u32[]{:S(2)}) copy-start(f32[16,64,128]{2,1,0:T(8,128)} %copy-done.12) | copy-start | bytes 1572868
where the time goes:
time: 150 us; the launch traced here: 149 us
  local copies, waits for them, and re-layouts  37.7 us (25%)
  matrix products  28.3 us (19%)
  starting transfers between devices  27.6 us (18%)
  blocking collectives  23.9 us (16%)
  other arithmetic  20.2 us (13%)
  waiting for transfers between devices  11.2 us (7%)
    dot_general x3, matrix products, per_device(): applied = jnp.einsum('rak,rkc->rac', blocks, gathered, precision=hp)  25 us
    all_to_all x1, blocking collectives, per_device(): lax.all_to_all(timed, 'space', split_axis=0, concat_axis=1, tiled=True)  23.9 us
    ppermute x6, starting transfers between devices, from_behind(): lax.ppermute(value, axis, [(source, source + steps) for source in range(l...  20.1 us
    gather x3, local copies, waits for them, and re-layouts, per_device(): gathered = widened[columns].reshape(br_local, SLOTS * BS, width)  16 us
    all_to_all x1, waiting for transfers between devices, per_device(): lax.all_to_all(source, 'space', split_axis=1, concat_axis=0, tiled=True)  10.9 us
    gather x3, local copies, waits for them, and re-layouts, per_device(): send_up = iterate[rows_up]  7.71 us
    all_to_all x1, starting transfers between devices, per_device(): lax.all_to_all(source, 'space', split_axis=1, concat_axis=0, tiled=True)  7.52 us
    gather x3, local copies, waits for them, and re-layouts, per_device(): send_down = iterate[rows_down]  6.43 us
  transfers between devices with their start and end apart: 7, of which 2 were waited for; matrix products, arithmetic and copies ran while one was open for 9% of the time, Pallas kernels for 0%

commit v1 on v0

v1 whole, which is shorter than its diff:
```python
import functools

import jax
import jax.numpy as jnp
import numpy as np
from jax import lax
from jax.experimental import pallas as pl
from jax.experimental.pallas import tpu as pltpu
from jax.sharding import PartitionSpec as P

BS = 64
SLOTS = 7
SHIFT_SCALE = 2.0
DIAG_CENTER = 4.0
LANES = 128
TERMS = 4
VMEM = pl.BlockSpec(memory_space=pltpu.VMEM)
SMEM = pl.BlockSpec(memory_space=pltpu.SMEM)


def time_filters(length):
    phase = np.exp(-2j * np.pi * np.arange(length) / length)
    step = 1.0 / (DIAG_CENTER + SHIFT_SCALE * (1.0 - phase))
    apart = np.arange(length)[:, None] - np.arange(length)[None, :]
    return [np.fft.ifft(step ** (m + 1)).real[apart % length] for m in range(TERMS)]


def halves(value):
    high = value.astype(jnp.bfloat16)
    return high, (value - high.astype(jnp.float32)).astype(jnp.bfloat16)


def mm(left, right):
    return jnp.dot(left, right, preferred_element_type=jnp.float32)


def mm_split(left, right_high, right_low):
    rows = left.shape[0]
    high, low = halves(left)
    both = mm(jnp.concatenate([high, low], axis=0), right_high)
    return both[:rows] + both[rows:] + mm(high, right_low)


def filter_mm(table, value):
    rows = table.shape[0] // 2
    high, low = halves(value)
    both = mm(table, high)
    return both[:rows] + both[rows:] + mm(table[:rows], low)


def build_kernel(count, me_ref, columns_ref, blocks_ref, high_ref, low_ref, full_ref):
    rows, size, _ = blocks_ref.shape
    halo = (full_ref.shape[0] // size - rows) // 2
    me = me_ref[0]
    even = lax.rem(me, 2) == 0
    full_ref[...] = jnp.zeros_like(full_ref)
    lane = lax.broadcasted_iota(jnp.int32, (size, 2 * size), 1)
    inner = lax.broadcasted_iota(jnp.int32, (size, 2 * size), 0)
    for pair in range(rows // 2):
        lanes = slice(pair * 2 * size, (pair + 1) * 2 * size)
        across = blocks_ref[2 * pair : 2 * pair + 2].reshape(2 * size, SLOTS * size).T
        for slot in range(SLOTS):
            piece = -across[slot * size : (slot + 1) * size]
            if slot == 0:
                piece = piece + jnp.where(lax.rem(lane, size) == inner, DIAG_CENTER, 0.0)
            for half in range(2):
                column = columns_ref[2 * pair + half, slot]
                kept = jnp.where(lane // size == half, piece, 0.0)
                if slot == 1:
                    column = jnp.where(even, column + halo, column)
                    kept = jnp.where(me == 0, 0.0, kept)
                if slot == 2:
                    column = jnp.where(even, column - halo, column)
                    kept = jnp.where(me == count - 1, 0.0, kept)
                at = pl.ds(pl.multiple_of(column * size, size), size)
                full_ref[at, lanes] += kept
    for start in range(0, full_ref.shape[0], size):
        high, low = halves(full_ref[start : start + size])
        high_ref[start : start + size] = high
        low_ref[start : start + size] = low


def pick(value_ref, rows_ref, out_ref):
    times, size = value_ref.shape[0], BS
    lane = lax.broadcasted_iota(jnp.int32, (times, 2 * size), 1)
    for pair in range(rows_ref.shape[0] // 2):
        parts = []
        for half in range(2):
            row = rows_ref[2 * pair + half]
            at = pl.ds(pl.multiple_of((row // 2) * 2 * size, 2 * size), 2 * size)
            tile = value_ref[:, at]
            parts.append(jnp.where(lax.rem(row, 2) == half, tile, pltpu.roll(tile, size, 1)))
        out_ref[:, pair * 2 * size : (pair + 1) * 2 * size] = jnp.where(lane < size, parts[0], parts[1])


def pick_both(me_ref, up_ref, down_ref, value_ref, inner_ref, outer_ref):
    even = lax.rem(me_ref[0], 2) == 0

    @pl.when(even)
    def _():
        pick(value_ref, up_ref, inner_ref)
        pick(value_ref, down_ref, outer_ref)

    @pl.when(jnp.logical_not(even))
    def _():
        pick(value_ref, down_ref, inner_ref)
        pick(value_ref, up_ref, outer_ref)


def first_kernel(me_ref, up_ref, down_ref, value_ref, inner_ref, outer_ref):
    pick_both(me_ref, up_ref, down_ref, value_ref, inner_ref, outer_ref)


def own_kernel(value_ref, high_ref, low_ref, out_ref):
    own = value_ref.shape[1]
    out_ref[...] = mm_split(value_ref[...], high_ref[:own], low_ref[:own])


def halo_product(inner_ref, outer_ref, high_ref, low_ref):
    both = jnp.concatenate([inner_ref[...], outer_ref[...]], axis=1)
    own = high_ref.shape[0] - both.shape[1]
    return mm_split(both, high_ref[own:], low_ref[own:])


def halo_kernel(me_ref, up_ref, down_ref, part_ref, from_inner, from_outer, high_ref, low_ref, out_ref, inner_ref, outer_ref):
    out_ref[...] = part_ref[...] + halo_product(from_inner, from_outer, high_ref, low_ref)
    pick_both(me_ref, up_ref, down_ref, out_ref, inner_ref, outer_ref)


def halo_last_kernel(me_ref, up_ref, down_ref, part_ref, from_inner, from_outer, high_ref, low_ref, table_ref, out_ref, inner_ref, outer_ref):
    value = part_ref[...] + halo_product(from_inner, from_outer, high_ref, low_ref)
    out_ref[...] = value
    pick_both(me_ref, up_ref, down_ref, out_ref, inner_ref, outer_ref)
    inner_ref[...] = filter_mm(table_ref[...], inner_ref[...])
    outer_ref[...] = filter_mm(table_ref[...], outer_ref[...])


def second_own_kernel(value_ref, start_ref, high_ref, low_ref, table0_ref, table1_ref, out_ref, total_ref):
    own_kernel(value_ref, high_ref, low_ref, out_ref)
    total_ref[...] = filter_mm(table0_ref[...], start_ref[...]) + filter_mm(table1_ref[...], value_ref[...])


def third_own_kernel(value_ref, total_ref, high_ref, low_ref, table2_ref, table3_ref, out_ref):
    own = value_ref.shape[1]
    value = value_ref[...]
    filtered = filter_mm(table3_ref[...], value)
    out_ref[...] = (
        total_ref[...] + filter_mm(table2_ref[...], value) + mm_split(filtered, high_ref[:own], low_ref[:own])
    )


def close_kernel(part_ref, from_inner, from_outer, high_ref, low_ref, out_ref):
    out_ref[...] = part_ref[...] + halo_product(from_inner, from_outer, high_ref, low_ref)


def call(kernel, outs, name, scratch=(), flops=1 << 28, specs=None):
    return pl.pallas_call(
        kernel,
        out_shape=outs,
        in_specs=specs,
        out_specs=jax.tree.map(lambda _: VMEM, outs),
        scratch_shapes=scratch,
        name=name,
        compiler_params=pltpu.CompilerParams(vmem_limit_bytes=32 << 20),
        cost_estimate=pl.CostEstimate(flops=flops, bytes_accessed=4 << 20, transcendentals=0),
    )


def per_device(source, blocks, columns, rows_up, rows_down):
    count = lax.axis_size("space")
    rows, halo = blocks.shape[0], rows_up.shape[0]
    own, width = rows * BS, halo * BS
    times = source.shape[0] * count
    me = lax.axis_index("space").reshape(1)
    f32 = lambda *shape: jax.ShapeDtypeStruct(shape, jnp.float32)
    bf16 = lambda *shape: jax.ShapeDtypeStruct(shape, jnp.bfloat16)
    tables = [
        jnp.concatenate(halves(jnp.asarray(table, jnp.float32)), axis=0) for table in time_filters(times)
    ]
    inner_pairs = [(i, i ^ 1) for i in range(count)]
    outer_pairs = [pair for i in range(1, count - 1, 2) for pair in ((i, i + 1), (i + 1, i))]

    def swap(inner, outer):
        return lax.ppermute(inner, "space", inner_pairs), lax.ppermute(outer, "space", outer_pairs)

    start = lax.all_to_all(source, "space", split_axis=1, concat_axis=0, tiled=True)
    high, low = call(
        functools.partial(build_kernel, count),
        (bf16(own + 2 * width, own), bf16(own + 2 * width, own)),
        "operator",
        scratch=[pltpu.VMEM((own + 2 * width, own), jnp.float32)],
        specs=[SMEM, SMEM, VMEM],
    )(me, columns, blocks)
    lists = (me, rows_up, rows_down)
    sent = (f32(times, width), f32(times, width))
    value = f32(times, own)

    inner, outer = call(first_kernel, sent, "first_rows", specs=[SMEM] * 3 + [VMEM])(*lists, start)
    inner, outer = swap(inner, outer)
    part = call(own_kernel, value, "own_1", specs=[VMEM] * 3)(start, high, low)
    once, inner, outer = call(halo_kernel, (value, *sent), "halo_1", specs=[SMEM] * 3 + [VMEM] * 5)(
        *lists, part, inner, outer, high, low
    )
    inner, outer = swap(inner, outer)
    part, total = call(second_own_kernel, (value, value), "own_2", specs=[VMEM] * 6)(
        once, start, high, low, tables[0], tables[1]
    )
    twice, inner, outer = call(halo_last_kernel, (value, *sent), "halo_2", specs=[SMEM] * 3 + [VMEM] * 6)(
        *lists, part, inner, outer, high, low, tables[3]
    )
    inner, outer = swap(inner, outer)
    part = call(third_own_kernel, value, "own_3", specs=[VMEM] * 6)(twice, total, high, low, tables[2], tables[3])
    timed = call(close_kernel, value, "halo_3", specs=[VMEM] * 5)(part, inner, outer, high, low)
    return lax.all_to_all(timed, "space", split_axis=0, concat_axis=1, tiled=True)


def solution(mesh):
    placed = (
        P("space", "group"),
        P(("group", "space"), None, None),
        P(("group", "space"), None),
        P(("group", "space")),
        P(("group", "space")),
    )
    return jax.shard_map(
        per_device, mesh=mesh, in_specs=placed, out_specs=P("space", "group"), check_vma=False
    )
```

time: 150 us -> 72.4 us (0.48)
  local copies, waits for them, and re-layouts: 37.7 us -> 4.5 us
  matrix products: 28.3 us -> 0 us
  other arithmetic: 20.2 us -> 0 us
  Pallas kernels: 0 us -> 11.4 us
  starting transfers between devices: 27.6 us -> 16.6 us
  waiting for transfers between devices: 11.2 us -> 14.5 us
    gather x9 -> x0, local copies, waits for them, and re-layouts: 30.1 us -> none  [the longest x3 16 us: per_device(): gathered = widened[columns].reshape(br_local, SLOTS * BS, width)]
    dot_general x5 -> x0, matrix products: 28.3 us -> none  [the longest x3 25 us: per_device(): applied = jnp.einsum('rak,rkc->rac', blocks, gathered, precision=hp)]
    pallas_call x0 -> x8, Pallas kernels: none -> 11.4 us  [the longest x1 3.38 us: per_device(): call(functools.partial(build_kernel, count), (bf16(own + 2 * width, own),...]
    ppermute x6, starting transfers between devices: 20.1 us -> 9.24 us  [the longest x3 7.26 us: swap(): lax.ppermute(inner, 'space', inner_pairs)]
    concatenate x4 -> x0, other arithmetic: 6.43 us -> none  [the longest x3 5.38 us: per_device(): widened = jnp.concatenate([iterate, below, above], axis=0)]
    sub x6 -> x0, other arithmetic: 6.19 us -> none  [full_mul(): factor_re * val_re - factor_im * val_im]
    add x3 -> x0, other arithmetic: 4.29 us -> none  [the longest x2 2.21 us: per_device(): iterate + full_mul(step_re, step_im, spectrum - (applied + full_mul(shift...]
    all_to_all x1, waiting for transfers between devices: 10.9 us -> 14.5 us  [per_device(): lax.all_to_all(source, 'space', split_axis=1, concat_axis=0, tiled=True)]
  transfers between devices with their start and end apart: 7 -> 7, of which waited for: 2 -> 1; matrix products, arithmetic and copies ran while one was open for 9% -> 1% of each run, Pallas kernels for 0% -> 10%
where the time goes in v1:
time: 72.4 us; the launch traced here: 72 us
  blocking collectives  24.8 us (34%)
  starting transfers between devices  16.6 us (23%)
  waiting for transfers between devices  14.5 us (20%)
  Pallas kernels  11.4 us (16%)
  local copies, waits for them, and re-layouts  4.5 us (6%)
    all_to_all x1, blocking collectives, per_device(): lax.all_to_all(timed, 'space', split_axis=0, concat_axis=1, tiled=True)  24.8 us
    all_to_all x1, waiting for transfers between devices, per_device(): lax.all_to_all(source, 'space', split_axis=1, concat_axis=0, tiled=True)  14.5 us
    all_to_all x1, starting transfers between devices, per_device(): lax.all_to_all(source, 'space', split_axis=1, concat_axis=0, tiled=True)  7.39 us
    ppermute x3, starting transfers between devices, swap(): lax.ppermute(inner, 'space', inner_pairs)  7.26 us
    unnamed x20, local copies, waits for them, and re-layouts  4.5 us
    pallas_call x1, Pallas kernels, per_device(): call(functools.partial(build_kernel, count), (bf16(own + 2 * width, own),...  3.38 us
    ppermute x3, starting transfers between devices, swap(): lax.ppermute(outer, 'space', outer_pairs)  1.98 us
    pallas_call x1, Pallas kernels, per_device(): call(halo_last_kernel, (value, *sent), 'halo_2', specs=[SMEM] * 3 + [VMEM...  1.58 us
  transfers between devices with their start and end apart: 7, of which 1 were waited for; matrix products, arithmetic and copies ran while one was open for 1% of the time, Pallas kernels for 10%

profile of v1, /device:TPU:0, one launch (start us, length us, event | category | flops | bytes accessed | tf_op | source)
XLA Modules:
  0.0 72.0 jit_solution(7690404630788436234)
XLA Ops:
  0.0 7.4 %all-to-all-start = ((f32[8,16,1024]{2,0,1:T(8,128)}), f32[8,16,1024]{2,0,1:T(8,128)S(1)}, u32[]{:S(2)}, u32[]{:S(2)}) async-start(f32[8,16,1024]{2,0,1:T(8,128)} %bitcast.14), calls=%async_computation | async-start | bytes 1048576 | tf_op jit(solution)/shard_map/all_to_all | solution.py:186
  7.4 14.5 %all-to-all-done = f32[8,16,1024]{2,0,1:T(8,128)S(1)} async-done(((f32[8,16,1024]{2,0,1:T(8,128)}), f32[8,16,1024]{2,0,1:T(8,128)S(1)}, u32[]{:S(2)}, u32[]{:S(2)}) %all-to-all-start) | async-done | bytes 524320 | tf_op jit(solution)/shard_map/all_to_all | solution.py:186
  21.9 0.0 copy-start.5
  21.9 0.7 copy-done.5
  22.5 0.0 copy-start.7
  22.5 0.7 copy-done.7
  23.2 0.8 %first_rows.1 = (f32[128,256]{1,0:T(8,128)S(1)}, f32[128,256]{1,0:T(8,128)S(1)}) custom-call(s32[1]{0:T(128)} %bitcast.me_ref, s32[4]{0:T(128)S(1)} %copy-done.5, s32[4]{0:T(128)S(1)} %copy-done.7, f32[128,1024]{1,0:T(8,128)S(1)} %bitcast.9), custom_call_target="tpu_custom_call" | custom-call | flops 268435456 | bytes 4194304 | tf_op jit(solution)/shard_map/first_rows/pallas_call | solution.py:198
  23.9 0.1 collective-permute-start
  24.0 0.7 collective-permute-start.1
  24.7 0.8 %copy.10.columns_ref = s32[16,7]{1,0:T(8,128)S(1)} copy(s32[16,7]{0,1:T(8,128)} %param.11) | data formatting | bytes 896 | tf_op args[2]
  25.5 0.0 copy-start
  25.5 1.6 %copy-done = f32[16,64,448]{2,1,0:T(8,128)S(1)} copy-done((f32[16,64,448]{2,1,0:T(8,128)S(1)}, f32[16,64,448]{2,1,0:T(8,128)}, u32[]{:S(2)}) %copy-start) | copy-done | bytes 1835032
  27.1 3.4 %operator.1 = (bf16[1536,1024]{1,0:T(8,128)(2,1)S(1)}, bf16[1536,1024]{1,0:T(8,128)(2,1)S(1)}) custom-call(s32[1]{0:T(128)} %bitcast.me_ref, s32[16,7]{1,0:T(8,128)S(1)} %copy.10.columns_ref, f32[16,64,448]{2,1,0:T(8,128)S(1)} %copy-done), custom_call_target="tpu_custom_call" | custom-call | flops 268435456 | bytes 4194304 | tf_op jit(solution)/shard_map/operator/pallas_call | solution.py:187
  30.4 0.0 copy-start.6
  30.5 0.0 copy-start.8
  30.5 1.0 %own_1.1.part_ref = f32[128,1024]{1,0:T(8,128)S(1)} custom-call(f32[128,1024]{1,0:T(8,128)S(1)} %bitcast.10, bf16[1536,1024]{1,0:T(8,128)(2,1)S(1)} %get-tuple-element.17.high_ref, bf16[1536,1024]{1,0:T(8,128)(2,1)S(1)} %get-tuple-element.18.low_ref), custom_call_target="tpu_custom_call" | custom-call | flops 268435456 | bytes 4194304 | tf_op jit(solution)/shard_map/own_1/pallas_call | solution.py:200
  31.4 0.0 copy-start.3
  31.5 0.0 copy-start.4
  31.5 0.0 collective-permute-done.from_inner
  31.5 0.0 collective-permute-done.1.from_outer
  31.5 0.0 copy-done.6
  31.5 0.0 copy-done.8
  31.5 1.3 %halo_1.1 = (f32[128,1024]{1,0:T(8,128)S(1)}, f32[128,256]{1,0:T(8,128)S(1)}, f32[128,256]{1,0:T(8,128)S(1)}) custom-call(s32[1]{0:T(128)} %bitcast.me_ref, s32[4]{0:T(128)S(1)} %copy-done.6, s32[4]{0:T(128)S(1)} %copy-done.8, f32[128,1024]{1,0:T(8,128)S(1)} %own_1.1.part_ref, f32[128,256]{1,0:T(8,128)S(1)} %collective-permute-done.from_inner, ...), custom_call_target="tpu_custom_call" | custom-call | flops 268435456 | bytes 4194304 | tf_op jit(solution)/shard_map/halo_1/pallas_call | solution.py:201
  32.9 2.6 %collective-permute-start.2 = (f32[128,256]{1,0:T(8,128)S(1)}, f32[128,256]{1,0:T(8,128)S(1)}, u32[]{:S(2)}, u32[]{:S(2)}) collective-permute-start(f32[128,256]{1,0:T(8,128)S(1)} %get-tuple-element.23), channel_id=1, source_target_pairs={{0,1},{1,0},{2,3},{3,2},{4,5},{5,4},{6,7},{7,6},{8,9},{9,8},{10,11... | collective-permute-start | bytes 393224 | tf_op jit(solution)/shard_map/ppermute | solution.py:184
  35.4 0.7 collective-permute-start.3
  36.1 0.0 copy-done.3
  36.1 0.0 copy-done.4
  36.1 0.0 copy-start.1
  36.1 1.4 %own_2.1 = (f32[128,1024]{1,0:T(8,128)S(1)}, f32[128,1024]{1,0:T(8,128)S(1)}) custom-call(f32[128,1024]{1,0:T(8,128)S(1)} %get-tuple-element.21.value_ref, f32[128,1024]{1,0:T(8,128)S(1)} %bitcast.11, bf16[1536,1024]{1,0:T(8,128)(2,1)S(1)} %get-tuple-element.17.high_ref, bf16[1536,1024]{1,0:T(8,128)(2,1)S(1)} %get-tuple-element.18.low_ref, ...), custom_call_target="tpu_custom_call" | custom-call | flops 268435456 | bytes 4194304 | tf_op jit(solution)/shard_map/own_2/pallas_call | solution.py:205
  37.5 0.0 collective-permute-done.2.from_inner
  37.5 0.0 collective-permute-done.3.from_outer
  37.5 0.0 copy-done.1
  37.5 0.0 copy-start.2
  37.6 1.6 %halo_2.1 = (f32[128,1024]{1,0:T(8,128)S(1)}, f32[128,256]{1,0:T(8,128)S(1)}, f32[128,256]{1,0:T(8,128)S(1)}) custom-call(s32[1]{0:T(128)} %bitcast.me_ref, s32[4]{0:T(128)S(1)} %copy-done.6, s32[4]{0:T(128)S(1)} %copy-done.8, f32[128,1024]{1,0:T(8,128)S(1)} %get-tuple-element.22.part_ref, f32[128,256]{1,0:T(8,128)S(1)} %collective-permute-done.2.from_inner, ...), custom_call_target="tpu_custom_call" | custom-call | flops 268435456 | bytes 4194304 | tf_op jit(solution)/shard_map/halo_2/pallas_call | solution.py:208
  39.1 4.6 %collective-permute-start.4 = (f32[128,256]{1,0:T(8,128)S(1)}, f32[128,256]{1,0:T(8,128)S(1)}, u32[]{:S(2)}, u32[]{:S(2)}) collective-permute-start(f32[128,256]{1,0:T(8,128)S(1)} %get-tuple-element.27), channel_id=1, source_target_pairs={{0,1},{1,0},{2,3},{3,2},{4,5},{5,4},{6,7},{7,6},{8,9},{9,8},{10,11... | collective-permute-start | bytes 393224 | tf_op jit(solution)/shard_map/ppermute | solution.py:184
  43.8 0.7 collective-permute-start.5
  44.4 0.0 copy-done.2
  44.4 1.4 %own_3.1.part_ref = f32[128,1024]{1,0:T(8,128)S(1)} custom-call(f32[128,1024]{1,0:T(8,128)S(1)} %get-tuple-element.25.value_ref, f32[128,1024]{1,0:T(8,128)S(1)} %get-tuple-element.26.total_ref, bf16[1536,1024]{1,0:T(8,128)(2,1)S(1)} %get-tuple-element.17.high_ref, bf16[1536,1024]{1,0:T(8,128)(2,1)S(1)} %get-tuple-element.18.low_ref, ...), custom_call_target="tpu_custom_call" | custom-call | flops 268435456 | bytes 4194304 | tf_op jit(solution)/shard_map/own_3/pallas_call | solution.py:212
  45.8 0.0 collective-permute-done.4.from_inner
  45.8 0.0 collective-permute-done.5.from_outer
  45.9 0.6 halo_3.1
  46.4 24.8 %all_to_all.38 = f32[16,8,1024]{2,1,0:T(8,128)S(1)} all-to-all(f32[16,8,1024]{2,1,0:T(8,128)S(1)} %bitcast.12), channel_id=1, replica_groups=mesh['group'=2,'space'=16] {'space'}, dimensions={0} | all-to-all | bytes 1048576 | tf_op jit(solution)/shard_map/all_to_all | solution.py:214
  71.2 0.8 %copy.12 = f32[8,16384]{1,0:T(8,128)} copy(f32[8,16384]{1,0:T(8,128)S(1)} %bitcast.13) | data formatting | bytes 1048576
Async XLA Ops:
  0.0 21.9 %all-to-all-start = ((f32[8,16,1024]{2,0,1:T(8,128)}), f32[8,16,1024]{2,0,1:T(8,128)S(1)}, u32[]{:S(2)}, u32[]{:S(2)}) async-start(f32[8,16,1024]{2,0,1:T(8,128)} %bitcast.14), calls=%async_computation | async-start | bytes 1048576 | tf_op jit(solution)/shard_map/all_to_all | solution.py:186
  21.9 0.7 copy-start.5
  22.5 0.7 copy-start.7
  23.9 7.5 %collective-permute-start = (f32[128,256]{1,0:T(8,128)S(1)}, f32[128,256]{1,0:T(8,128)S(1)}, u32[]{:S(2)}, u32[]{:S(2)}) collective-permute-start(f32[128,256]{1,0:T(8,128)S(1)} %get-tuple-element.19), channel_id=1, source_target_pairs={{0,1},{1,0},{2,3},{3,2},{4,5},{5,4},{6,7},{7,6},{8,9},{9,8},{10,11... | collective-permute-start | bytes 393224 | tf_op jit(solution)/shard_map/ppermute | solution.py:184
  24.0 7.5 %collective-permute-start.1 = (f32[128,256]{1,0:T(8,128)S(1)}, f32[128,256]{1,0:T(8,128)S(1)}, u32[]{:S(2)}, u32[]{:S(2)}) collective-permute-start(f32[128,256]{1,0:T(8,128)S(1)} %get-tuple-element.20), channel_id=1, source_target_pairs={{1,2},{2,1},{3,4},{4,3},{5,6},{6,5},{7,8},{8,7},{9,10},{10,9},{11,... | collective-permute-start | bytes 393224 | tf_op jit(solution)/shard_map/ppermute | solution.py:184
  25.5 1.6 %copy-start = (f32[16,64,448]{2,1,0:T(8,128)S(1)}, f32[16,64,448]{2,1,0:T(8,128)}, u32[]{:S(2)}) copy-start(f32[16,64,448]{2,1,0:T(8,128)} %blocks_ref.1) | copy-start | bytes 5505028
  30.4 1.1 %copy-start.6 = (s32[4]{0:T(128)S(1)}, s32[4]{0:T(128)}, u32[]{:S(2)}) copy-start(s32[4]{0:T(128)} %up_ref.5) | copy-start | bytes 52
  30.5 1.0 %copy-start.8 = (s32[4]{0:T(128)S(1)}, s32[4]{0:T(128)}, u32[]{:S(2)}) copy-start(s32[4]{0:T(128)} %down_ref.5) | copy-start | bytes 52
  31.4 4.6 %copy-start.3 = (bf16[256,128]{1,0:T(8,128)(2,1)S(1)}, bf16[256,128]{1,0:T(8,128)(2,1)}, u32[]{:S(2)}) copy-start(bf16[256,128]{1,0:T(8,128)(2,1)} %constant.30.table1_ref) | copy-start | bytes 196612
  31.5 4.6 %copy-start.4 = (bf16[256,128]{1,0:T(8,128)(2,1)S(1)}, bf16[256,128]{1,0:T(8,128)(2,1)}, u32[]{:S(2)}) copy-start(bf16[256,128]{1,0:T(8,128)(2,1)} %constant.25.table0_ref) | copy-start | bytes 196612
  32.9 4.7 %collective-permute-start.2 = (f32[128,256]{1,0:T(8,128)S(1)}, f32[128,256]{1,0:T(8,128)S(1)}, u32[]{:S(2)}, u32[]{:S(2)}) collective-permute-start(f32[128,256]{1,0:T(8,128)S(1)} %get-tuple-element.23), channel_id=1, source_target_pairs={{0,1},{1,0},{2,3},{3,2},{4,5},{5,4},{6,7},{7,6},{8,9},{9,8},{10,11... | collective-permute-start | bytes 393224 | tf_op jit(solution)/shard_map/ppermute | solution.py:184
  35.4 2.1 %collective-permute-start.3 = (f32[128,256]{1,0:T(8,128)S(1)}, f32[128,256]{1,0:T(8,128)S(1)}, u32[]{:S(2)}, u32[]{:S(2)}) collective-permute-start(f32[128,256]{1,0:T(8,128)S(1)} %get-tuple-element.24), channel_id=1, source_target_pairs={{1,2},{2,1},{3,4},{4,3},{5,6},{6,5},{7,8},{8,7},{9,10},{10,9},{11,... | collective-permute-start | bytes 393224 | tf_op jit(solution)/shard_map/ppermute | solution.py:184
  36.1 1.4 %copy-start.1 = (bf16[256,128]{1,0:T(8,128)(2,1)S(1)}, bf16[256,128]{1,0:T(8,128)(2,1)}, u32[]{:S(2)}) copy-start(bf16[256,128]{1,0:T(8,128)(2,1)} %constant.35.table_ref.table3_ref) | copy-start | bytes 196612
  37.5 6.9 %copy-start.2 = (bf16[256,128]{1,0:T(8,128)(2,1)S(1)}, bf16[256,128]{1,0:T(8,128)(2,1)}, u32[]{:S(2)}) copy-start(bf16[256,128]{1,0:T(8,128)(2,1)} %constant.40.table2_ref) | copy-start | bytes 196612
  39.1 6.7 %collective-permute-start.4 = (f32[128,256]{1,0:T(8,128)S(1)}, f32[128,256]{1,0:T(8,128)S(1)}, u32[]{:S(2)}, u32[]{:S(2)}) collective-permute-start(f32[128,256]{1,0:T(8,128)S(1)} %get-tuple-element.27), channel_id=1, source_target_pairs={{0,1},{1,0},{2,3},{3,2},{4,5},{5,4},{6,7},{7,6},{8,9},{9,8},{10,11... | collective-permute-start | bytes 393224 | tf_op jit(solution)/shard_map/ppermute | solution.py:184
  43.8 2.1 %collective-permute-start.5 = (f32[128,256]{1,0:T(8,128)S(1)}, f32[128,256]{1,0:T(8,128)S(1)}, u32[]{:S(2)}, u32[]{:S(2)}) collective-permute-start(f32[128,256]{1,0:T(8,128)S(1)} %get-tuple-element.28), channel_id=1, source_target_pairs={{1,2},{2,1},{3,4},{4,3},{5,6},{6,5},{7,8},{8,7},{9,10},{10,9},{11,... | collective-permute-start | bytes 393224 | tf_op jit(solution)/shard_map/ppermute | solution.py:184

commit v2 on v1

v2 whole, which is shorter than its diff:
```python
import functools

import jax
import jax.numpy as jnp
import numpy as np
from jax import lax
from jax.experimental import pallas as pl
from jax.experimental.pallas import tpu as pltpu
from jax.sharding import PartitionSpec as P

BS = 64
SLOTS = 7
SHIFT_SCALE = 2.0
DIAG_CENTER = 4.0
TERMS = 4
VMEM = pl.BlockSpec(memory_space=pltpu.VMEM)
SMEM = pl.BlockSpec(memory_space=pltpu.SMEM)
ANY = pl.BlockSpec(memory_space=pl.ANY)


def time_filters(length):
    phase = np.exp(-2j * np.pi * np.arange(length) / length)
    step = 1.0 / (DIAG_CENTER + SHIFT_SCALE * (1.0 - phase))
    apart = np.arange(length)[:, None] - np.arange(length)[None, :]
    return [np.fft.ifft(step ** (m + 1)).real[apart % length] for m in range(TERMS)]


def halves(value):
    high = value.astype(jnp.bfloat16)
    return high, (value - high.astype(jnp.float32)).astype(jnp.bfloat16)


def mm(left, right):
    return jnp.dot(left, right, preferred_element_type=jnp.float32)


def mm_split(left, right_high, right_low):
    rows = left.shape[0]
    high, low = halves(left)
    both = mm(jnp.concatenate([high, low], axis=0), right_high)
    return both[:rows] + both[rows:] + mm(high, right_low)


def filter_mm(table, value):
    rows = table.shape[0] // 2
    high, low = halves(value)
    both = mm(table, high)
    return both[:rows] + both[rows:] + mm(table[:rows], low)


def chosen(even, up_ref, down_ref, index, halo):
    first = jnp.where(even, up_ref[index % halo], down_ref[index % halo])
    second = jnp.where(even, down_ref[index % halo], up_ref[index % halo])
    return first if index < halo else second


def build_kernel(
    count, me_ref, columns_ref, up_ref, down_ref, blocks_in,
    high_ref, low_ref, sent_high_ref, sent_low_ref, place_ref, table_ref, blocks_ref, block_sems,
):
    rows, size, _ = blocks_ref.shape
    halo = up_ref.shape[0]
    pieces = [
        pltpu.make_async_copy(
            blocks_in.at[pl.ds(2 * pair, 2)], blocks_ref.at[pl.ds(2 * pair, 2)], block_sems.at[pair]
        )
        for pair in range(rows // 2)
    ]
    for copy in pieces:
        copy.start()
    me = me_ref[0]
    even = lax.rem(me, 2) == 0
    sent = [chosen(even, up_ref, down_ref, index, halo) for index in range(2 * halo)]
    for index in range(2 * halo):
        table_ref[SLOTS, index] = sent[index]
    for row in range(rows):
        for slot in range(SLOTS):
            column = columns_ref[slot, row]
            if slot in (1, 2):
                column = jnp.where(even, column + (halo if slot == 1 else -halo), column)
            table_ref[slot, row] = column
    lane = lax.broadcasted_iota(jnp.int32, (size, 2 * size), 1)
    inner = lax.broadcasted_iota(jnp.int32, (size, 2 * size), 0)
    for pair in range(rows // 2):
        pieces[pair].wait()
        lanes = slice(pair * 2 * size, (pair + 1) * 2 * size)
        across = -blocks_ref[2 * pair : 2 * pair + 2].reshape(2 * size, SLOTS * size).T
        part = [across[slot * size : (slot + 1) * size] for slot in range(SLOTS)]
        part[0] = part[0] + jnp.where(lax.rem(lane, size) == inner, DIAG_CENTER, 0.0)
        part[1] = jnp.where(me == 0, 0.0, part[1])
        part[2] = jnp.where(me == count - 1, 0.0, part[2])
        for later in range(3, SLOTS):
            for sooner in (0, *range(3, later)):
                same = [columns_ref[later, 2 * pair + half] == columns_ref[sooner, 2 * pair + half] for half in range(2)]
                moved = jnp.where(lane < size, same[0].astype(jnp.int32), same[1].astype(jnp.int32)) > 0
                part[sooner] = part[sooner] + jnp.where(moved, part[later], 0.0)
                part[later] = jnp.where(moved, 0.0, part[later])
        for slot in range(SLOTS):
            high, low = halves(part[slot])
            high_ref[slot * size : (slot + 1) * size, lanes] = high
            low_ref[slot * size : (slot + 1) * size, lanes] = low
    wide = lax.broadcasted_iota(jnp.int32, (2 * size, 2 * size), 1)
    for pair in range(halo):
        lanes = slice(pair * 2 * size, (pair + 1) * 2 * size)
        for whole_ref, few_ref in ((high_ref, sent_high_ref), (low_ref, sent_low_ref)):
            parts = []
            for half in range(2):
                row = sent[2 * pair + half]
                at = pl.ds(pl.multiple_of((row // 2) * 2 * size, 2 * size), 2 * size)
                tile = whole_ref[size : 3 * size, at].astype(jnp.float32)
                parts.append(jnp.where(lax.rem(row, 2) == half, tile, pltpu.roll(tile, size, 1)))
            few_ref[:, lanes] = jnp.where(wide < size, parts[0], parts[1]).astype(jnp.bfloat16)
        across = lax.broadcasted_iota(jnp.int32, (place_ref.shape[0], 2 * size), 1)
        place_ref[:, lanes] = jnp.where(across < size, sent[2 * pair], sent[2 * pair + 1] - 1) * size + across


def store_sent(value, inner_ref, outer_ref):
    width = inner_ref.shape[1]
    inner_ref[...] = value[:, :width]
    outer_ref[...] = value[:, width:]


def picked(value, pick_ref):
    high, low = halves(value)
    rows = high.shape[0]
    both = mm(jnp.concatenate([high, low], axis=0), pick_ref[...])
    return both[:rows] + both[rows:]


def first_kernel(value_ref, place_ref, inner_ref, outer_ref, pick_ref):
    down = lax.broadcasted_iota(jnp.int32, pick_ref.shape, 0)
    pick_ref[...] = jnp.where(down == place_ref[0:1, :], 1.0, 0.0).astype(jnp.bfloat16)
    store_sent(picked(value_ref[...], pick_ref), inner_ref, outer_ref)


def own_first_kernel(
    value_ref, blocks_high, blocks_low, sent_high, sent_low, pick_ref, table_in,
    out_ref, sent_ref, high_ref, low_ref, halo_high, halo_low, table_ref, sem,
):
    times, own = value_ref.shape
    size = BS
    rows = own // size
    copy = pltpu.make_async_copy(table_in, table_ref, sem)
    copy.start()
    for ref in (high_ref, low_ref, halo_high, halo_low):
        ref[...] = jnp.zeros_like(ref)
    copy.wait()
    for slot in reversed(range(SLOTS)):
        for row in range(rows):
            at = pl.ds(pl.multiple_of(table_ref[slot, row] * size, size), size)
            lanes = slice(row * size, (row + 1) * size)
            high_ref[at, lanes] = blocks_high[slot * size : (slot + 1) * size, lanes]
            low_ref[at, lanes] = blocks_low[slot * size : (slot + 1) * size, lanes]
    for index in range(sent_high.shape[1] // size):
        row = table_ref[SLOTS, index]
        lanes = slice(index * size, (index + 1) * size)
        for slot in (1, 2):
            at = pl.ds(pl.multiple_of((table_ref[slot, row] - rows) * size, size), size)
            halo_high[at, lanes] = sent_high[(slot - 1) * size : slot * size, lanes]
            halo_low[at, lanes] = sent_low[(slot - 1) * size : slot * size, lanes]
    out_ref[...] = mm_split(value_ref[...], high_ref[:own], low_ref[:own])
    sent_ref[...] = picked(out_ref[...], pick_ref)


def halo_product(inner_ref, outer_ref, high, low):
    both = jnp.concatenate([inner_ref[...], outer_ref[...]], axis=1)
    return mm_split(both, high, low)


def send_kernel(part_ref, from_inner, from_outer, halo_high, halo_low, inner_ref, outer_ref):
    value = part_ref[...] + halo_product(from_inner, from_outer, halo_high[...], halo_low[...])
    store_sent(value, inner_ref, outer_ref)


def send_last_kernel(part_ref, from_inner, from_outer, halo_high, halo_low, table_ref, inner_ref, outer_ref):
    value = part_ref[...] + halo_product(from_inner, from_outer, halo_high[...], halo_low[...])
    store_sent(filter_mm(table_ref[...], value), inner_ref, outer_ref)


def own_second_kernel(
    start_ref, part_ref, from_inner, from_outer, high_ref, low_ref, pick_ref, table0_ref, table1_ref,
    out_ref, sent_ref, total_ref,
):
    own = part_ref.shape[1]
    value = part_ref[...] + halo_product(from_inner, from_outer, high_ref[own:], low_ref[own:])
    out_ref[...] = mm_split(value, high_ref[:own], low_ref[:own])
    sent_ref[...] = picked(out_ref[...], pick_ref)
    total_ref[...] = filter_mm(table0_ref[...], start_ref[...]) + filter_mm(table1_ref[...], value)


def own_third_kernel(part_ref, from_inner, from_outer, total_ref, high_ref, low_ref, table2_ref, table3_ref, out_ref):
    own = part_ref.shape[1]
    value = part_ref[...] + halo_product(from_inner, from_outer, high_ref[own:], low_ref[own:])
    filtered = filter_mm(table3_ref[...], value)
    out_ref[...] = (
        total_ref[...] + filter_mm(table2_ref[...], value) + mm_split(filtered, high_ref[:own], low_ref[:own])
    )


def close_kernel(part_ref, from_inner, from_outer, high_ref, low_ref, out_ref):
    own = part_ref.shape[1]
    out_ref[...] = part_ref[...] + halo_product(from_inner, from_outer, high_ref[own:], low_ref[own:])


def call(kernel, outs, name, ins, out_specs=None, scratch=(), moved=4 << 20):
    return pl.pallas_call(
        kernel,
        out_shape=outs,
        in_specs=ins,
        out_specs=jax.tree.map(lambda _: VMEM, outs) if out_specs is None else out_specs,
        scratch_shapes=scratch,
        name=name,
        compiler_params=pltpu.CompilerParams(vmem_limit_bytes=32 << 20),
        cost_estimate=pl.CostEstimate(flops=1 << 28, bytes_accessed=moved, transcendentals=0),
    )


def per_device(source, blocks, columns, rows_up, rows_down):
    count = lax.axis_size("space")
    rows, halo = blocks.shape[0], rows_up.shape[0]
    own, width = rows * BS, halo * BS
    times = source.shape[0] * count
    me = lax.axis_index("space").reshape(1)
    f32 = lambda *shape: jax.ShapeDtypeStruct(shape, jnp.float32)
    bf16 = lambda *shape: jax.ShapeDtypeStruct(shape, jnp.bfloat16)
    tables = [
        jnp.concatenate(halves(jnp.asarray(table, jnp.float32)), axis=0) for table in time_filters(times)
    ]
    inner_pairs = [(i, i ^ 1) for i in range(count)]
    outer_pairs = [pair for i in range(1, count - 1, 2) for pair in ((i, i + 1), (i + 1, i))]

    def swap(inner, outer):
        return lax.ppermute(inner, "space", inner_pairs), lax.ppermute(outer, "space", outer_pairs)

    start = lax.all_to_all(source, "space", split_axis=1, concat_axis=0, tiled=True)
    side = own + 2 * width
    dma = pltpu.SemaphoreType.DMA
    *blocked, place, table = call(
        functools.partial(build_kernel, count),
        (
            *[bf16(SLOTS * BS, own)] * 2,
            *[bf16(2 * BS, 2 * width)] * 2,
            jax.ShapeDtypeStruct((8, 2 * width), jnp.int32),
            jax.ShapeDtypeStruct((SLOTS + 1, rows), jnp.int32),
        ),
        "operator",
        [SMEM] * 4 + [ANY],
        (VMEM,) * 5 + (SMEM,),
        scratch=[pltpu.VMEM(blocks.shape, jnp.float32), dma((rows // 2,))],
        moved=16 << 20,
    )(me, columns.T, rows_up, rows_down, blocks)
    sent = (f32(times, width), f32(times, width))
    value, ahead = f32(times, own), f32(times, 2 * width)

    inner, outer, pick = call(first_kernel, (*sent, bf16(own, 2 * width)), "send_0", [VMEM] * 2)(start, place)
    inner, outer = swap(inner, outer)
    part, part_sent, high, low, *halo_parts = call(
        own_first_kernel,
        (value, ahead, *[bf16(side, own)] * 2, *[bf16(2 * width, 2 * width)] * 2),
        "own_1",
        [VMEM] * 6 + [ANY],
        scratch=[pltpu.SMEM((SLOTS + 1, rows), jnp.int32), dma],
    )(start, *blocked, pick, table)
    next_inner, next_outer = call(send_kernel, sent, "send_1", [VMEM] * 5)(part_sent, inner, outer, *halo_parts)
    next_inner, next_outer = swap(next_inner, next_outer)
    part, part_sent, total = call(own_second_kernel, (value, ahead, value), "own_2", [VMEM] * 9)(
        start, part, inner, outer, high, low, pick, tables[0], tables[1]
    )
    inner, outer = next_inner, next_outer
    next_inner, next_outer = call(send_last_kernel, sent, "send_2", [VMEM] * 6)(
        part_sent, inner, outer, *halo_parts, tables[3]
    )
    next_inner, next_outer = swap(next_inner, next_outer)
    part = call(own_third_kernel, value, "own_3", [VMEM] * 8)(part, inner, outer, total, high, low, tables[2], tables[3])
    timed = call(close_kernel, value, "close", [VMEM] * 5)(part, next_inner, next_outer, high, low)
    return lax.all_to_all(timed, "space", split_axis=0, concat_axis=1, tiled=True)


def solution(mesh):
    placed = (
        P("space", "group"),
        P(("group", "space"), None, None),
        P(("group", "space"), None),
        P(("group", "space")),
        P(("group", "space")),
    )
    return jax.shard_map(
        per_device, mesh=mesh, in_specs=placed, out_specs=P("space", "group"), check_vma=False
    )
```

time: 72.4 us -> 66.4 us (0.917)
  waiting for transfers between devices: 14.5 us -> 7.82 us
    all_to_all x1, waiting for transfers between devices: 14.5 us -> 7.8 us  [per_device(): lax.all_to_all(source, 'space', split_axis=1, concat_axis=0, tiled=True)]
    unnamed x20 -> x17, local copies, waits for them, and re-layouts: 4.5 us -> 4.4 us
  transfers between devices with their start and end apart: 7 -> 7, of which waited for: 1 -> 1; matrix products, arithmetic and copies ran while one was open for 1% -> 0% of each run, Pallas kernels for 10% -> 15%
where the time goes in v2:
time: 66.4 us; the launch traced here: 66 us
  blocking collectives  25.1 us (38%)
  starting transfers between devices  16.9 us (25%)
  Pallas kernels  11.6 us (17%)
  waiting for transfers between devices  7.82 us (12%)
  local copies, waits for them, and re-layouts  4.4 us (7%)
    all_to_all x1, blocking collectives, per_device(): lax.all_to_all(timed, 'space', split_axis=0, concat_axis=1, tiled=True)  25.1 us
    all_to_all x1, waiting for transfers between devices, per_device(): lax.all_to_all(source, 'space', split_axis=1, concat_axis=0, tiled=True)  7.8 us
    ppermute x3, starting transfers between devices, swap(): lax.ppermute(inner, 'space', inner_pairs)  7.54 us
    all_to_all x1, starting transfers between devices, per_device(): lax.all_to_all(source, 'space', split_axis=1, concat_axis=0, tiled=True)  7.38 us
    unnamed x17, local copies, waits for them, and re-layouts  4.4 us
    pallas_call x1, Pallas kernels, per_device(): call(functools.partial(build_kernel, count), (*[bf16(SLOTS * BS, own)] *...  3.03 us
    pallas_call x1, Pallas kernels, per_device(): call(own_first_kernel, (value, ahead, *[bf16(side, own)] * 2, *[bf16(2 *...  2.63 us
    pallas_call x1, Pallas kernels, per_device(): call(own_second_kernel, (value, ahead, value), 'own_2', [VMEM] * 9)  2.11 us
  transfers between devices with their start and end apart: 7, of which 1 were waited for; matrix products, arithmetic and copies ran while one was open for 0% of the time, Pallas kernels for 15%

profile of v2, /device:TPU:0, one launch (start us, length us, event | category | flops | bytes accessed | tf_op | source)
XLA Modules:
  0.0 66.0 jit_solution(3581475258103944546)
XLA Ops:
  0.0 7.4 %all-to-all-start = ((f32[8,16,1024]{2,0,1:T(8,128)}), f32[8,16,1024]{2,0,1:T(8,128)S(1)}, u32[]{:S(2)}, u32[]{:S(2)}) async-start(f32[8,16,1024]{2,0,1:T(8,128)} %bitcast.16), calls=%async_computation | async-start | bytes 1048576 | tf_op jit(solution)/shard_map/all_to_all | solution.py:235
  7.4 0.0 copy-start
  7.4 1.6 %copy-done = f32[16,64,448]{2,1,0:T(8,128)S(1)} copy-done((f32[16,64,448]{2,1,0:T(8,128)S(1)}, f32[16,64,448]{2,1,0:T(8,128)}, u32[]{:S(2)}) %copy-start) | copy-done | bytes 1835032
  9.0 0.0 copy-start.5
  9.0 0.7 %copy-done.5 = s32[16,7]{0,1:T(8,128)S(1)} copy-done((s32[16,7]{0,1:T(8,128)S(1)}, s32[16,7]{0,1:T(8,128)}, u32[]{:S(2)}) %copy-start.5) | copy-done | bytes 472
  9.7 0.0 copy-start.6
  9.7 0.7 copy-done.6
  10.3 0.0 copy-start.7
  10.3 0.7 copy-done.7
  11.0 3.0 %operator.1 = (bf16[448,1024]{1,0:T(8,128)(2,1)S(1)}, bf16[448,1024]{1,0:T(8,128)(2,1)S(1)}, bf16[128,512]{1,0:T(8,128)(2,1)S(1)}, bf16[128,512]{1,0:T(8,128)(2,...) custom-call(s32[1]{0:T(128)} %bitcast.4.me_ref, s32[7,16]{1,0:T(8,128)S(1)} %bitcast.14, s32[4]{0:T(128)S(1)} %copy-done.6, ...), custom_call_target="tpu_custom_call" | custom-call | flops 268435456 | bytes 16777216 | tf_op jit(solution)/shard_map/operator/pallas_call | solution.py:238
  14.0 0.0 copy-start.3
  14.0 0.0 copy-start.4
  14.1 7.8 %all-to-all-done = f32[8,16,1024]{2,0,1:T(8,128)S(1)} async-done(((f32[8,16,1024]{2,0,1:T(8,128)}), f32[8,16,1024]{2,0,1:T(8,128)S(1)}, u32[]{:S(2)}, u32[]{:S(2)}) %all-to-all-start) | async-done | bytes 524320 | tf_op jit(solution)/shard_map/all_to_all | solution.py:235
  21.9 0.5 send_0.1
  22.3 0.1 collective-permute-start
  22.4 0.7 %collective-permute-start.1 = (f32[128,256]{1,0:T(8,128)S(1)}, f32[128,256]{1,0:T(8,128)S(1)}, u32[]{:S(2)}, u32[]{:S(2)}) collective-permute-start(f32[128,256]{1,0:T(8,128)S(1)} %get-tuple-element.36), channel_id=1, source_target_pairs={{1,2},{2,1},{3,4},{4,3},{5,6},{6,5},{7,8},{8,7},{9,10},{10,9},{11,... | collective-permute-start | bytes 393224 | tf_op jit(solution)/shard_map/ppermute | solution.py:233
  23.1 2.6 %own_1.1 = (f32[128,1024]{1,0:T(8,128)S(1)}, f32[128,512]{1,0:T(8,128)S(1)}, bf16[1536,1024]{1,0:T(8,128)(2,1)S(1)}, bf16[1536,1024]{1,0:T(8,128)(2,1)S(1)}, bf1...) custom-call(f32[128,1024]{1,0:T(8,128)S(1)} %bitcast.11, bf16[448,1024]{1,0:T(8,128)(2,1)S(1)} %get-tuple-element.27.blocks_high, ...), custom_call_target="tpu_custom_call" | custom-call | flops 268435456 | bytes 4194304 | tf_op jit(solution)/shard_map/own_1/pallas_call | solution.py:257
  25.7 0.0 collective-permute-done.from_inner
  25.7 0.0 collective-permute-done.1.from_outer
  25.7 0.4 send_1.1
  26.1 3.5 %collective-permute-start.2 = (f32[128,256]{1,0:T(8,128)S(1)}, f32[128,256]{1,0:T(8,128)S(1)}, u32[]{:S(2)}, u32[]{:S(2)}) collective-permute-start(f32[128,256]{1,0:T(8,128)S(1)} %get-tuple-element.43), channel_id=1, source_target_pairs={{0,1},{1,0},{2,3},{3,2},{4,5},{5,4},{6,7},{7,6},{8,9},{9,8},{10,11... | collective-permute-start | bytes 393224 | tf_op jit(solution)/shard_map/ppermute | solution.py:233
  29.6 0.7 collective-permute-start.3
  30.3 0.0 copy-done.3
  30.3 0.0 copy-done.4
  30.3 0.0 copy-start.1
  30.3 0.0 copy-start.2
  30.3 2.1 %own_2.1 = (f32[128,1024]{1,0:T(8,128)S(1)}, f32[128,512]{1,0:T(8,128)S(1)}, f32[128,1024]{1,0:T(8,128)S(1)}) custom-call(f32[128,1024]{1,0:T(8,128)S(1)} %bitcast.12, f32[128,1024]{1,0:T(8,128)S(1)} %get-tuple-element.34.part_ref, f32[128,256]{1,0:T(8,128)S(1)} %collective-permute-done.from_inner, f32[128,256]{1,0:T(8,128)S(1)} %collective-permute-done.1.from_outer, ...), custom_call_target="tpu_custom_call" | custom-call | flops 268435456 | bytes 4194304 | tf_op jit(solution)/shard_map/own_2/pallas_call | solution.py:266
  32.4 0.0 collective-permute-done.2.from_inner
  32.4 0.0 collective-permute-done.3.from_outer
  32.5 0.0 copy-done.1
  32.5 0.6 send_2.1
  33.1 4.0 %collective-permute-start.4 = (f32[128,256]{1,0:T(8,128)S(1)}, f32[128,256]{1,0:T(8,128)S(1)}, u32[]{:S(2)}, u32[]{:S(2)}) collective-permute-start(f32[128,256]{1,0:T(8,128)S(1)} %get-tuple-element.47), channel_id=1, source_target_pairs={{0,1},{1,0},{2,3},{3,2},{4,5},{5,4},{6,7},{7,6},{8,9},{9,8},{10,11... | collective-permute-start | bytes 393224 | tf_op jit(solution)/shard_map/ppermute | solution.py:233
  37.0 0.7 collective-permute-start.5
  37.7 0.0 copy-done.2
  37.7 1.9 %own_3.1.part_ref = f32[128,1024]{1,0:T(8,128)S(1)} custom-call(f32[128,1024]{1,0:T(8,128)S(1)} %get-tuple-element.39.part_ref, f32[128,256]{1,0:T(8,128)S(1)} %collective-permute-done.2.from_inner, f32[128,256]{1,0:T(8,128)S(1)} %collective-permute-done.3.from_outer, f32[128,1024]{1,0:T(8,128)S(1)} %get-tuple-element.45.total_ref, ...), custom_call_target="tpu_custom_call" | custom-call | flops 268435456 | bytes 4194304 | tf_op jit(solution)/shard_map/own_3/pallas_call | solution.py:274
  39.6 0.0 collective-permute-done.4.from_inner
  39.6 0.0 collective-permute-done.5.from_outer
  39.6 0.6 close.1
  40.2 25.1 %all_to_all.38 = f32[16,8,1024]{2,1,0:T(8,128)S(1)} all-to-all(f32[16,8,1024]{2,1,0:T(8,128)S(1)} %bitcast.13), channel_id=1, replica_groups=mesh['group'=2,'space'=16] {'space'}, dimensions={0} | all-to-all | bytes 1048576 | tf_op jit(solution)/shard_map/all_to_all | solution.py:276
  65.2 0.8 %copy.11 = f32[8,16384]{1,0:T(8,128)} copy(f32[8,16384]{1,0:T(8,128)S(1)} %bitcast.15) | data formatting | bytes 1048576
Async XLA Ops:
  0.0 21.9 %all-to-all-start = ((f32[8,16,1024]{2,0,1:T(8,128)}), f32[8,16,1024]{2,0,1:T(8,128)S(1)}, u32[]{:S(2)}, u32[]{:S(2)}) async-start(f32[8,16,1024]{2,0,1:T(8,128)} %bitcast.16), calls=%async_computation | async-start | bytes 1048576 | tf_op jit(solution)/shard_map/all_to_all | solution.py:235
  7.4 1.6 %copy-start = (f32[16,64,448]{2,1,0:T(8,128)S(1)}, f32[16,64,448]{2,1,0:T(8,128)}, u32[]{:S(2)}) copy-start(f32[16,64,448]{2,1,0:T(8,128)} %blocks_in.1) | copy-start | bytes 5505028
  9.0 0.7 %copy-start.5 = (s32[16,7]{0,1:T(8,128)S(1)}, s32[16,7]{0,1:T(8,128)}, u32[]{:S(2)}) copy-start(s32[16,7]{0,1:T(8,128)} %param.11) | copy-start | bytes 1348
  9.7 0.7 copy-start.6
  10.3 0.7 copy-start.7
  14.0 16.2 %copy-start.3 = (bf16[256,128]{1,0:T(8,128)(2,1)S(1)}, bf16[256,128]{1,0:T(8,128)(2,1)}, u32[]{:S(2)}) copy-start(bf16[256,128]{1,0:T(8,128)(2,1)} %constant.30.table1_ref) | copy-start | bytes 196612
  14.0 16.2 %copy-start.4 = (bf16[256,128]{1,0:T(8,128)(2,1)S(1)}, bf16[256,128]{1,0:T(8,128)(2,1)}, u32[]{:S(2)}) copy-start(bf16[256,128]{1,0:T(8,128)(2,1)} %constant.25.table0_ref) | copy-start | bytes 196612
  22.3 3.4 %collective-permute-start = (f32[128,256]{1,0:T(8,128)S(1)}, f32[128,256]{1,0:T(8,128)S(1)}, u32[]{:S(2)}, u32[]{:S(2)}) collective-permute-start(f32[128,256]{1,0:T(8,128)S(1)} %get-tuple-element.35), channel_id=1, source_target_pairs={{0,1},{1,0},{2,3},{3,2},{4,5},{5,4},{6,7},{7,6},{8,9},{9,8},{10,11... | collective-permute-start | bytes 393224 | tf_op jit(solution)/shard_map/ppermute | solution.py:233
  22.4 3.3 %collective-permute-start.1 = (f32[128,256]{1,0:T(8,128)S(1)}, f32[128,256]{1,0:T(8,128)S(1)}, u32[]{:S(2)}, u32[]{:S(2)}) collective-permute-start(f32[128,256]{1,0:T(8,128)S(1)} %get-tuple-element.36), channel_id=1, source_target_pairs={{1,2},{2,1},{3,4},{4,3},{5,6},{6,5},{7,8},{8,7},{9,10},{10,9},{11,... | collective-permute-start | bytes 393224 | tf_op jit(solution)/shard_map/ppermute | solution.py:233
  26.1 6.3 %collective-permute-start.2 = (f32[128,256]{1,0:T(8,128)S(1)}, f32[128,256]{1,0:T(8,128)S(1)}, u32[]{:S(2)}, u32[]{:S(2)}) collective-permute-start(f32[128,256]{1,0:T(8,128)S(1)} %get-tuple-element.43), channel_id=1, source_target_pairs={{0,1},{1,0},{2,3},{3,2},{4,5},{5,4},{6,7},{7,6},{8,9},{9,8},{10,11... | collective-permute-start | bytes 393224 | tf_op jit(solution)/shard_map/ppermute | solution.py:233
  29.6 2.8 %collective-permute-start.3 = (f32[128,256]{1,0:T(8,128)S(1)}, f32[128,256]{1,0:T(8,128)S(1)}, u32[]{:S(2)}, u32[]{:S(2)}) collective-permute-start(f32[128,256]{1,0:T(8,128)S(1)} %get-tuple-element.44), channel_id=1, source_target_pairs={{1,2},{2,1},{3,4},{4,3},{5,6},{6,5},{7,8},{8,7},{9,10},{10,9},{11,... | collective-permute-start | bytes 393224 | tf_op jit(solution)/shard_map/ppermute | solution.py:233
  30.3 2.2 %copy-start.1 = (bf16[256,128]{1,0:T(8,128)(2,1)S(1)}, bf16[256,128]{1,0:T(8,128)(2,1)}, u32[]{:S(2)}) copy-start(bf16[256,128]{1,0:T(8,128)(2,1)} %constant.40.table3_ref.table_ref) | copy-start | bytes 196612
  30.3 7.4 %copy-start.2 = (bf16[256,128]{1,0:T(8,128)(2,1)S(1)}, bf16[256,128]{1,0:T(8,128)(2,1)}, u32[]{:S(2)}) copy-start(bf16[256,128]{1,0:T(8,128)(2,1)} %constant.35.table2_ref) | copy-start | bytes 196612
  33.1 6.5 %collective-permute-start.4 = (f32[128,256]{1,0:T(8,128)S(1)}, f32[128,256]{1,0:T(8,128)S(1)}, u32[]{:S(2)}, u32[]{:S(2)}) collective-permute-start(f32[128,256]{1,0:T(8,128)S(1)} %get-tuple-element.47), channel_id=1, source_target_pairs={{0,1},{1,0},{2,3},{3,2},{4,5},{5,4},{6,7},{7,6},{8,9},{9,8},{10,11... | collective-permute-start | bytes 393224 | tf_op jit(solution)/shard_map/ppermute | solution.py:233
  37.0 2.6 %collective-permute-start.5 = (f32[128,256]{1,0:T(8,128)S(1)}, f32[128,256]{1,0:T(8,128)S(1)}, u32[]{:S(2)}, u32[]{:S(2)}) collective-permute-start(f32[128,256]{1,0:T(8,128)S(1)} %get-tuple-element.48), channel_id=1, source_target_pairs={{1,2},{2,1},{3,4},{4,3},{5,6},{6,5},{7,8},{8,7},{9,10},{10,9},{11,... | collective-permute-start | bytes 393224 | tf_op jit(solution)/shard_map/ppermute | solution.py:233

commit v3 on v2

--- a/solution.py
+++ b/solution.py
@@ -162,6 +162,11 @@
     sent_ref[...] = picked(out_ref[...], pick_ref)
 
 
+def halo_once(inner_ref, outer_ref, high):
+    both = jnp.concatenate([inner_ref[...], outer_ref[...]], axis=1)
+    return mm(both.astype(jnp.bfloat16), high)
+
+
 def halo_product(inner_ref, outer_ref, high, low):
     both = jnp.concatenate([inner_ref[...], outer_ref[...]], axis=1)
     return mm_split(both, high, low)
@@ -174,7 +179,8 @@
 
 def send_last_kernel(part_ref, from_inner, from_outer, halo_high, halo_low, table_ref, inner_ref, outer_ref):
     value = part_ref[...] + halo_product(from_inner, from_outer, halo_high[...], halo_low[...])
-    store_sent(filter_mm(table_ref[...], value), inner_ref, outer_ref)
+    table = table_ref[: value.shape[0]]
+    store_sent(mm(table, value.astype(jnp.bfloat16)), inner_ref, outer_ref)
 
 
 def own_second_kernel(
@@ -197,9 +203,9 @@
     )
 
 
-def close_kernel(part_ref, from_inner, from_outer, high_ref, low_ref, out_ref):
+def close_kernel(part_ref, from_inner, from_outer, high_ref, out_ref):
     own = part_ref.shape[1]
-    out_ref[...] = part_ref[...] + halo_product(from_inner, from_outer, high_ref[own:], low_ref[own:])
+    out_ref[...] = part_ref[...] + halo_once(from_inner, from_outer, high_ref[own:])
 
 
 def call(kernel, outs, name, ins, out_specs=None, scratch=(), moved=4 << 20):
@@ -227,10 +233,18 @@
         jnp.concatenate(halves(jnp.asarray(table, jnp.float32)), axis=0) for table in time_filters(times)
     ]
     inner_pairs = [(i, i ^ 1) for i in range(count)]
-    outer_pairs = [pair for i in range(1, count - 1, 2) for pair in ((i, i + 1), (i + 1, i))]
+    groups = lax.axis_size("group")
+    outer_pairs = [
+        (group * count + i, group * count + j)
+        for group in range(groups)
+        for pair in range(1, count - 1, 2)
+        for i, j in ((pair, pair + 1), (pair + 1, pair))
+    ]
+    if groups % 2 == 0:
+        outer_pairs += [(group * count + i, (group ^ 1) * count + i) for group in range(groups) for i in (0, count - 1)]
 
     def swap(inner, outer):
-        return lax.ppermute(inner, "space", inner_pairs), lax.ppermute(outer, "space", outer_pairs)
+        return lax.ppermute(inner, "space", inner_pairs), lax.ppermute(outer, ("group", "space"), outer_pairs)
 
     start = lax.all_to_all(source, "space", split_axis=1, concat_axis=0, tiled=True)
     side = own + 2 * width
@@ -272,7 +286,7 @@
     )
     next_inner, next_outer = swap(next_inner, next_outer)
     part = call(own_third_kernel, value, "own_3", [VMEM] * 8)(part, inner, outer, total, high, low, tables[2], tables[3])
-    timed = call(close_kernel, value, "close", [VMEM] * 5)(part, next_inner, next_outer, high, low)
+    timed = call(close_kernel, value, "close", [VMEM] * 4)(part, next_inner, next_outer, high)
     return lax.all_to_all(timed, "space", split_axis=0, concat_axis=1, tiled=True)
 
 

time: 66.4 us -> 60.4 us (0.910)
  blocking collectives: 25.1 us -> 20.4 us
  starting transfers between devices: 16.9 us -> 12.4 us
  waiting for transfers between devices: 7.82 us -> 11.6 us
    ppermute x3, starting transfers between devices: 7.54 us -> 0.44 us  [swap(): lax.ppermute(inner, 'space', inner_pairs)]
    all_to_all x1, blocking collectives: 25.1 us -> 20.4 us  [per_device(): lax.all_to_all(timed, 'space', split_axis=0, concat_axis=1, tiled=True)]
    ppermute x3, waiting for transfers between devices: 0.01 us -> 3.76 us  [swap(): lax.ppermute(outer, ('group', 'space'), outer_pairs)]
    ppermute x3, starting transfers between devices: 1.98 us -> 4.54 us  [swap(): lax.ppermute(outer, ('group', 'space'), outer_pairs)]
  transfers between devices with their start and end apart: 7 -> 7, of which waited for: 1 -> 4; matrix products, arithmetic and copies ran while one was open for 0% -> 0% of each run, Pallas kernels for 15% -> 16%
where the time goes in v3:
time: 60.4 us; the launch traced here: 60.1 us
  blocking collectives  20.4 us (34%)
  starting transfers between devices  12.4 us (21%)
  waiting for transfers between devices  11.6 us (19%)
  Pallas kernels  11.3 us (19%)
  local copies, waits for them, and re-layouts  4.4 us (7%)
    all_to_all x1, blocking collectives, per_device(): lax.all_to_all(timed, 'space', split_axis=0, concat_axis=1, tiled=True)  20.4 us
    all_to_all x1, waiting for transfers between devices, per_device(): lax.all_to_all(source, 'space', split_axis=1, concat_axis=0, tiled=True)  7.8 us
    all_to_all x1, starting transfers between devices, per_device(): lax.all_to_all(source, 'space', split_axis=1, concat_axis=0, tiled=True)  7.38 us
    ppermute x3, starting transfers between devices, swap(): lax.ppermute(outer, ('group', 'space'), outer_pairs)  4.54 us
    unnamed x17, local copies, waits for them, and re-layouts  4.4 us
    ppermute x3, waiting for transfers between devices, swap(): lax.ppermute(outer, ('group', 'space'), outer_pairs)  3.76 us
    pallas_call x1, Pallas kernels, per_device(): call(functools.partial(build_kernel, count), (*[bf16(SLOTS * BS, own)] *...  3.03 us
    pallas_call x1, Pallas kernels, per_device(): call(own_first_kernel, (value, ahead, *[bf16(side, own)] * 2, *[bf16(2 *...  2.62 us
  transfers between devices with their start and end apart: 7, of which 4 were waited for; matrix products, arithmetic and copies ran while one was open for 0% of the time, Pallas kernels for 16%

profile of v3, /device:TPU:0, one launch (start us, length us, event | category | flops | bytes accessed | tf_op | source)
XLA Modules:
  0.0 60.1 jit_solution(17069351599133273363)
XLA Ops:
  0.0 7.4 %all-to-all-start = ((f32[8,16,1024]{2,0,1:T(8,128)}), f32[8,16,1024]{2,0,1:T(8,128)S(1)}, u32[]{:S(2)}, u32[]{:S(2)}) async-start(f32[8,16,1024]{2,0,1:T(8,128)} %bitcast.16), calls=%async_computation | async-start | bytes 1048576 | tf_op jit(solution)/shard_map/all_to_all | solution.py:249
  7.4 0.0 copy-start
  7.4 1.6 %copy-done = f32[16,64,448]{2,1,0:T(8,128)S(1)} copy-done((f32[16,64,448]{2,1,0:T(8,128)S(1)}, f32[16,64,448]{2,1,0:T(8,128)}, u32[]{:S(2)}) %copy-start) | copy-done | bytes 1835032
  9.0 0.0 copy-start.5
  9.0 0.7 %copy-done.5 = s32[16,7]{0,1:T(8,128)S(1)} copy-done((s32[16,7]{0,1:T(8,128)S(1)}, s32[16,7]{0,1:T(8,128)}, u32[]{:S(2)}) %copy-start.5) | copy-done | bytes 472
  9.7 0.0 copy-start.6
  9.7 0.7 %copy-done.6 = s32[4]{0:T(128)S(1)} copy-done((s32[4]{0:T(128)S(1)}, s32[4]{0:T(128)}, u32[]{:S(2)}) %copy-start.6) | copy-done | bytes 40
  10.3 0.0 copy-start.7
  10.3 0.7 %copy-done.7 = s32[4]{0:T(128)S(1)} copy-done((s32[4]{0:T(128)S(1)}, s32[4]{0:T(128)}, u32[]{:S(2)}) %copy-start.7) | copy-done | bytes 40
  11.0 3.0 %operator.1 = (bf16[448,1024]{1,0:T(8,128)(2,1)S(1)}, bf16[448,1024]{1,0:T(8,128)(2,1)S(1)}, bf16[128,512]{1,0:T(8,128)(2,1)S(1)}, bf16[128,512]{1,0:T(8,128)(2,...) custom-call(s32[1]{0:T(128)} %bitcast.4.me_ref, s32[7,16]{1,0:T(8,128)S(1)} %bitcast.14, s32[4]{0:T(128)S(1)} %copy-done.6, ...), custom_call_target="tpu_custom_call" | custom-call | flops 268435456 | bytes 16777216 | tf_op jit(solution)/shard_map/operator/pallas_call | solution.py:252
  14.0 0.0 copy-start.3
  14.0 0.0 copy-start.4
  14.1 7.8 %all-to-all-done = f32[8,16,1024]{2,0,1:T(8,128)S(1)} async-done(((f32[8,16,1024]{2,0,1:T(8,128)}), f32[8,16,1024]{2,0,1:T(8,128)S(1)}, u32[]{:S(2)}, u32[]{:S(2)}) %all-to-all-start) | async-done | bytes 524320 | tf_op jit(solution)/shard_map/all_to_all | solution.py:249
  21.9 0.5 send_0.1
  22.3 0.1 collective-permute-start
  22.4 1.6 %collective-permute-start.1 = (f32[128,256]{1,0:T(8,128)S(1)}, f32[128,256]{1,0:T(8,128)S(1)}, u32[]{:S(2)}, u32[]{:S(2)}) collective-permute-start(f32[128,256]{1,0:T(8,128)S(1)} %get-tuple-element.36), channel_id=1, source_target_pairs={{1,2},{2,1},{3,4},{4,3},{5,6},{6,5},{7,8},{8,7},{9,10},{10,9},{11,... | collective-permute-start | bytes 393224 | tf_op jit(solution)/shard_map/ppermute | solution.py:247
  24.0 2.6 %own_1.1 = (f32[128,1024]{1,0:T(8,128)S(1)}, f32[128,512]{1,0:T(8,128)S(1)}, bf16[1536,1024]{1,0:T(8,128)(2,1)S(1)}, bf16[1536,1024]{1,0:T(8,128)(2,1)S(1)}, bf1...) custom-call(f32[128,1024]{1,0:T(8,128)S(1)} %bitcast.11, bf16[448,1024]{1,0:T(8,128)(2,1)S(1)} %get-tuple-element.27.blocks_high, ...), custom_call_target="tpu_custom_call" | custom-call | flops 268435456 | bytes 4194304 | tf_op jit(solution)/shard_map/own_1/pallas_call | solution.py:271
  26.6 0.0 collective-permute-done.from_inner
  26.6 0.8 %collective-permute-done.1.from_outer = f32[128,256]{1,0:T(8,128)S(1)} collective-permute-done((f32[128,256]{1,0:T(8,128)S(1)}, f32[128,256]{1,0:T(8,128)S(1)}, u32[]{:S(2)}, u32[]{:S(2)}) %collective-permute-start.1) | collective-permute-done | bytes 131104 | tf_op jit(solution)/shard_map/ppermute | solution.py:247
  27.4 0.4 send_1.1
  27.8 0.2 collective-permute-start.2
  28.0 1.5 %collective-permute-start.3 = (f32[128,256]{1,0:T(8,128)S(1)}, f32[128,256]{1,0:T(8,128)S(1)}, u32[]{:S(2)}, u32[]{:S(2)}) collective-permute-start(f32[128,256]{1,0:T(8,128)S(1)} %get-tuple-element.44), channel_id=1, source_target_pairs={{1,2},{2,1},{3,4},{4,3},{5,6},{6,5},{7,8},{8,7},{9,10},{10,9},{11,... | collective-permute-start | bytes 393224 | tf_op jit(solution)/shard_map/ppermute | solution.py:247
  29.5 0.0 copy-done.3
  29.5 0.0 copy-done.4
  29.5 0.0 copy-start.1
  29.5 0.0 copy-start.2
  29.5 2.1 %own_2.1 = (f32[128,1024]{1,0:T(8,128)S(1)}, f32[128,512]{1,0:T(8,128)S(1)}, f32[128,1024]{1,0:T(8,128)S(1)}) custom-call(f32[128,1024]{1,0:T(8,128)S(1)} %bitcast.12, f32[128,1024]{1,0:T(8,128)S(1)} %get-tuple-element.34.part_ref, f32[128,256]{1,0:T(8,128)S(1)} %collective-permute-done.from_inner, f32[128,256]{1,0:T(8,128)S(1)} %collective-permute-done.1.from_outer, ...), custom_call_target="tpu_custom_call" | custom-call | flops 268435456 | bytes 4194304 | tf_op jit(solution)/shard_map/own_2/pallas_call | solution.py:280
  31.6 0.0 collective-permute-done.2.from_inner
  31.6 1.3 %collective-permute-done.3.from_outer = f32[128,256]{1,0:T(8,128)S(1)} collective-permute-done((f32[128,256]{1,0:T(8,128)S(1)}, f32[128,256]{1,0:T(8,128)S(1)}, u32[]{:S(2)}, u32[]{:S(2)}) %collective-permute-start.3) | collective-permute-done | bytes 131104 | tf_op jit(solution)/shard_map/ppermute | solution.py:247
  33.0 0.0 copy-done.1
  33.0 0.5 send_2.1
  33.5 0.2 collective-permute-start.4
  33.7 1.5 %collective-permute-start.5 = (f32[128,256]{1,0:T(8,128)S(1)}, f32[128,256]{1,0:T(8,128)S(1)}, u32[]{:S(2)}, u32[]{:S(2)}) collective-permute-start(f32[128,256]{1,0:T(8,128)S(1)} %get-tuple-element.48), channel_id=1, source_target_pairs={{1,2},{2,1},{3,4},{4,3},{5,6},{6,5},{7,8},{8,7},{9,10},{10,9},{11,... | collective-permute-start | bytes 393224 | tf_op jit(solution)/shard_map/ppermute | solution.py:247
  35.2 0.0 copy-done.2
  35.2 1.9 %own_3.1.part_ref = f32[128,1024]{1,0:T(8,128)S(1)} custom-call(f32[128,1024]{1,0:T(8,128)S(1)} %get-tuple-element.39.part_ref, f32[128,256]{1,0:T(8,128)S(1)} %collective-permute-done.2.from_inner, f32[128,256]{1,0:T(8,128)S(1)} %collective-permute-done.3.from_outer, f32[128,1024]{1,0:T(8,128)S(1)} %get-tuple-element.45.total_ref, ...), custom_call_target="tpu_custom_call" | custom-call | flops 268435456 | bytes 4194304 | tf_op jit(solution)/shard_map/own_3/pallas_call | solution.py:288
  37.0 0.0 collective-permute-done.4.from_inner
  37.0 1.6 %collective-permute-done.5.from_outer = f32[128,256]{1,0:T(8,128)S(1)} collective-permute-done((f32[128,256]{1,0:T(8,128)S(1)}, f32[128,256]{1,0:T(8,128)S(1)}, u32[]{:S(2)}, u32[]{:S(2)}) %collective-permute-start.5) | collective-permute-done | bytes 131104 | tf_op jit(solution)/shard_map/ppermute | solution.py:247
  38.6 0.3 close.1
  39.0 20.4 %all_to_all.38 = f32[16,8,1024]{2,1,0:T(8,128)S(1)} all-to-all(f32[16,8,1024]{2,1,0:T(8,128)S(1)} %bitcast.13), channel_id=1, replica_groups=mesh['group'=2,'space'=16] {'space'}, dimensions={0} | all-to-all | bytes 1048576 | tf_op jit(solution)/shard_map/all_to_all | solution.py:290
  59.3 0.8 %copy.11 = f32[8,16384]{1,0:T(8,128)} copy(f32[8,16384]{1,0:T(8,128)S(1)} %bitcast.15) | data formatting | bytes 1048576
Async XLA Ops:
  0.0 21.9 %all-to-all-start = ((f32[8,16,1024]{2,0,1:T(8,128)}), f32[8,16,1024]{2,0,1:T(8,128)S(1)}, u32[]{:S(2)}, u32[]{:S(2)}) async-start(f32[8,16,1024]{2,0,1:T(8,128)} %bitcast.16), calls=%async_computation | async-start | bytes 1048576 | tf_op jit(solution)/shard_map/all_to_all | solution.py:249
  7.4 1.6 %copy-start = (f32[16,64,448]{2,1,0:T(8,128)S(1)}, f32[16,64,448]{2,1,0:T(8,128)}, u32[]{:S(2)}) copy-start(f32[16,64,448]{2,1,0:T(8,128)} %blocks_in.1) | copy-start | bytes 5505028
  9.0 0.7 %copy-start.5 = (s32[16,7]{0,1:T(8,128)S(1)}, s32[16,7]{0,1:T(8,128)}, u32[]{:S(2)}) copy-start(s32[16,7]{0,1:T(8,128)} %param.11) | copy-start | bytes 1348
  9.7 0.7 %copy-start.6 = (s32[4]{0:T(128)S(1)}, s32[4]{0:T(128)}, u32[]{:S(2)}) copy-start(s32[4]{0:T(128)} %up_ref.1) | copy-start | bytes 52
  10.3 0.7 %copy-start.7 = (s32[4]{0:T(128)S(1)}, s32[4]{0:T(128)}, u32[]{:S(2)}) copy-start(s32[4]{0:T(128)} %down_ref.1) | copy-start | bytes 52
  14.0 15.5 %copy-start.3 = (bf16[256,128]{1,0:T(8,128)(2,1)S(1)}, bf16[256,128]{1,0:T(8,128)(2,1)}, u32[]{:S(2)}) copy-start(bf16[256,128]{1,0:T(8,128)(2,1)} %constant.30.table1_ref) | copy-start | bytes 196612
  14.0 15.4 %copy-start.4 = (bf16[256,128]{1,0:T(8,128)(2,1)S(1)}, bf16[256,128]{1,0:T(8,128)(2,1)}, u32[]{:S(2)}) copy-start(bf16[256,128]{1,0:T(8,128)(2,1)} %constant.25.table0_ref) | copy-start | bytes 196612
  22.3 4.3 %collective-permute-start = (f32[128,256]{1,0:T(8,128)S(1)}, f32[128,256]{1,0:T(8,128)S(1)}, u32[]{:S(2)}, u32[]{:S(2)}) collective-permute-start(f32[128,256]{1,0:T(8,128)S(1)} %get-tuple-element.35), channel_id=1, source_target_pairs={{0,1},{1,0},{2,3},{3,2},{4,5},{5,4},{6,7},{7,6},{8,9},{9,8},{10,11... | collective-permute-start | bytes 393224 | tf_op jit(solution)/shard_map/ppermute | solution.py:247
  22.4 5.0 %collective-permute-start.1 = (f32[128,256]{1,0:T(8,128)S(1)}, f32[128,256]{1,0:T(8,128)S(1)}, u32[]{:S(2)}, u32[]{:S(2)}) collective-permute-start(f32[128,256]{1,0:T(8,128)S(1)} %get-tuple-element.36), channel_id=1, source_target_pairs={{1,2},{2,1},{3,4},{4,3},{5,6},{6,5},{7,8},{8,7},{9,10},{10,9},{11,... | collective-permute-start | bytes 393224 | tf_op jit(solution)/shard_map/ppermute | solution.py:247
  27.8 3.8 %collective-permute-start.2 = (f32[128,256]{1,0:T(8,128)S(1)}, f32[128,256]{1,0:T(8,128)S(1)}, u32[]{:S(2)}, u32[]{:S(2)}) collective-permute-start(f32[128,256]{1,0:T(8,128)S(1)} %get-tuple-element.43), channel_id=1, source_target_pairs={{0,1},{1,0},{2,3},{3,2},{4,5},{5,4},{6,7},{7,6},{8,9},{9,8},{10,11... | collective-permute-start | bytes 393224 | tf_op jit(solution)/shard_map/ppermute | solution.py:247
  28.0 5.0 %collective-permute-start.3 = (f32[128,256]{1,0:T(8,128)S(1)}, f32[128,256]{1,0:T(8,128)S(1)}, u32[]{:S(2)}, u32[]{:S(2)}) collective-permute-start(f32[128,256]{1,0:T(8,128)S(1)} %get-tuple-element.44), channel_id=1, source_target_pairs={{1,2},{2,1},{3,4},{4,3},{5,6},{6,5},{7,8},{8,7},{9,10},{10,9},{11,... | collective-permute-start | bytes 393224 | tf_op jit(solution)/shard_map/ppermute | solution.py:247
  29.5 3.5 %copy-start.1 = (bf16[256,128]{1,0:T(8,128)(2,1)S(1)}, bf16[256,128]{1,0:T(8,128)(2,1)}, u32[]{:S(2)}) copy-start(bf16[256,128]{1,0:T(8,128)(2,1)} %constant.40.table3_ref.table_ref) | copy-start | bytes 196612
  29.5 5.7 %copy-start.2 = (bf16[256,128]{1,0:T(8,128)(2,1)S(1)}, bf16[256,128]{1,0:T(8,128)(2,1)}, u32[]{:S(2)}) copy-start(bf16[256,128]{1,0:T(8,128)(2,1)} %constant.35.table2_ref) | copy-start | bytes 196612
  33.5 3.5 %collective-permute-start.4 = (f32[128,256]{1,0:T(8,128)S(1)}, f32[128,256]{1,0:T(8,128)S(1)}, u32[]{:S(2)}, u32[]{:S(2)}) collective-permute-start(f32[128,256]{1,0:T(8,128)S(1)} %get-tuple-element.47), channel_id=1, source_target_pairs={{0,1},{1,0},{2,3},{3,2},{4,5},{5,4},{6,7},{7,6},{8,9},{9,8},{10,11... | collective-permute-start | bytes 393224 | tf_op jit(solution)/shard_map/ppermute | solution.py:247
  33.7 5.0 %collective-permute-start.5 = (f32[128,256]{1,0:T(8,128)S(1)}, f32[128,256]{1,0:T(8,128)S(1)}, u32[]{:S(2)}, u32[]{:S(2)}) collective-permute-start(f32[128,256]{1,0:T(8,128)S(1)} %get-tuple-element.48), channel_id=1, source_target_pairs={{1,2},{2,1},{3,4},{4,3},{5,6},{6,5},{7,8},{8,7},{9,10},{10,9},{11,... | collective-permute-start | bytes 393224 | tf_op jit(solution)/shard_map/ppermute | solution.py:247

commit v4 on v3

--- a/solution.py
+++ b/solution.py
@@ -13,6 +13,7 @@
 SHIFT_SCALE = 2.0
 DIAG_CENTER = 4.0
 TERMS = 4
+SEND_ORDER = (5, 8, 12, 4, 9, 10, 6, 7, 14, 1, 15, 2, 11, 13, 3, 0)
 VMEM = pl.BlockSpec(memory_space=pltpu.VMEM)
 SMEM = pl.BlockSpec(memory_space=pltpu.SMEM)
 ANY = pl.BlockSpec(memory_space=pl.ANY)
@@ -23,6 +24,10 @@
     step = 1.0 / (DIAG_CENTER + SHIFT_SCALE * (1.0 - phase))
     apart = np.arange(length)[:, None] - np.arange(length)[None, :]
     return [np.fft.ifft(step ** (m + 1)).real[apart % length] for m in range(TERMS)]
+
+
+def send_order(count):
+    return list(SEND_ORDER) if count == len(SEND_ORDER) else list(range(count))
 
 
 def halves(value):
@@ -208,6 +213,22 @@
     out_ref[...] = part_ref[...] + halo_once(from_inner, from_outer, high_ref[own:])
 
 
+def store_kernel(order, value_ref, out_ref, sems):
+    step = value_ref.shape[1] // len(order)
+    copies = [
+        pltpu.make_async_copy(
+            value_ref.at[:, index * step : (index + 1) * step],
+            out_ref.at[:, sender * step : (sender + 1) * step],
+            sems.at[index],
+        )
+        for index, sender in enumerate(order)
+    ]
+    for copy in copies:
+        copy.start()
+    for copy in copies:
+        copy.wait()
+
+
 def call(kernel, outs, name, ins, out_specs=None, scratch=(), moved=4 << 20):
     return pl.pallas_call(
         kernel,
@@ -229,8 +250,10 @@
     me = lax.axis_index("space").reshape(1)
     f32 = lambda *shape: jax.ShapeDtypeStruct(shape, jnp.float32)
     bf16 = lambda *shape: jax.ShapeDtypeStruct(shape, jnp.bfloat16)
+    order = send_order(count)
+    told = np.arange(times).reshape(count, -1)[np.array(order)].reshape(-1)
     tables = [
-        jnp.concatenate(halves(jnp.asarray(table, jnp.float32)), axis=0) for table in time_filters(times)
+        jnp.concatenate(halves(jnp.asarray(table[told], jnp.float32)), axis=0) for table in time_filters(times)
     ]
     inner_pairs = [(i, i ^ 1) for i in range(count)]
     groups = lax.axis_size("group")
@@ -287,7 +310,17 @@
     next_inner, next_outer = swap(next_inner, next_outer)
     part = call(own_third_kernel, value, "own_3", [VMEM] * 8)(part, inner, outer, total, high, low, tables[2], tables[3])
     timed = call(close_kernel, value, "close", [VMEM] * 4)(part, next_inner, next_outer, high)
-    return lax.all_to_all(timed, "space", split_axis=0, concat_axis=1, tiled=True)
+    field = lax.all_to_all(
+        timed, "space", split_axis=0, concat_axis=1, tiled=True, axis_index_groups=[order]
+    )
+    return call(
+        functools.partial(store_kernel, order),
+        jax.ShapeDtypeStruct(field.shape, field.dtype),
+        "store",
+        [VMEM],
+        ANY,
+        scratch=[pltpu.SemaphoreType.DMA((count,))],
+    )(field)
 
 
 def solution(mesh):

time: 60.4 us -> 58.4 us (0.967)
  blocking collectives: 20.4 us -> 18.2 us
  Pallas kernels: 11.3 us -> 12.2 us
  local copies, waits for them, and re-layouts: 4.4 us -> 3.6 us
    all_to_all x1, blocking collectives: 20.4 us -> 18.2 us  [per_device(): lax.all_to_all(timed, 'space', split_axis=0, concat_axis=1, tiled=True, a...]
    pallas_call x0 -> x1, Pallas kernels: none -> 0.91 us  [per_device(): call(functools.partial(store_kernel, order), jax.ShapeDtypeStruct(field.s...]
    unnamed x17 -> x16, local copies, waits for them, and re-layouts: 4.4 us -> 3.6 us
  transfers between devices with their start and end apart: 7 -> 7, of which waited for: 4 -> 4; matrix products, arithmetic and copies ran while one was open for 0% -> 0% of each run, Pallas kernels for 16% -> 17%
where the time goes in v4:
time: 58.4 us; the launch traced here: 58.1 us
  blocking collectives  18.2 us (31%)
  starting transfers between devices  12.4 us (21%)
  Pallas kernels  12.2 us (21%)
  waiting for transfers between devices  11.6 us (20%)
  local copies, waits for them, and re-layouts  3.6 us (6%)
    all_to_all x1, blocking collectives, per_device(): lax.all_to_all(timed, 'space', split_axis=0, concat_axis=1, tiled=True, a...  18.2 us
    all_to_all x1, waiting for transfers between devices, per_device(): lax.all_to_all(source, 'space', split_axis=1, concat_axis=0, tiled=True)  7.8 us
    all_to_all x1, starting transfers between devices, per_device(): lax.all_to_all(source, 'space', split_axis=1, concat_axis=0, tiled=True)  7.38 us
    ppermute x3, starting transfers between devices, swap(): lax.ppermute(outer, ('group', 'space'), outer_pairs)  4.54 us
    ppermute x3, waiting for transfers between devices, swap(): lax.ppermute(outer, ('group', 'space'), outer_pairs)  3.76 us
    unnamed x16, local copies, waits for them, and re-layouts  3.6 us
    pallas_call x1, Pallas kernels, per_device(): call(functools.partial(build_kernel, count), (*[bf16(SLOTS * BS, own)] *...  3.03 us
    pallas_call x1, Pallas kernels, per_device(): call(own_first_kernel, (value, ahead, *[bf16(side, own)] * 2, *[bf16(2 *...  2.62 us
  transfers between devices with their start and end apart: 7, of which 4 were waited for; matrix products, arithmetic and copies ran while one was open for 0% of the time, Pallas kernels for 17%

profile of v4, /device:TPU:0, one launch (start us, length us, event | category | flops | bytes accessed | tf_op | source)
XLA Modules:
  0.0 58.1 jit_solution(2388598652524690080)
XLA Ops:
  0.0 7.4 %all-to-all-start = ((f32[8,16,1024]{2,0,1:T(8,128)}), f32[8,16,1024]{2,0,1:T(8,128)S(1)}, u32[]{:S(2)}, u32[]{:S(2)}) async-start(f32[8,16,1024]{2,0,1:T(8,128)} %bitcast.16), calls=%async_computation | async-start | bytes 1048576 | tf_op jit(solution)/shard_map/all_to_all | solution.py:272
  7.4 0.0 copy-start
  7.4 1.6 %copy-done = f32[16,64,448]{2,1,0:T(8,128)S(1)} copy-done((f32[16,64,448]{2,1,0:T(8,128)S(1)}, f32[16,64,448]{2,1,0:T(8,128)}, u32[]{:S(2)}) %copy-start) | copy-done | bytes 1835032
  9.0 0.0 copy-start.5
  9.0 0.7 %copy-done.5 = s32[16,7]{0,1:T(8,128)S(1)} copy-done((s32[16,7]{0,1:T(8,128)S(1)}, s32[16,7]{0,1:T(8,128)}, u32[]{:S(2)}) %copy-start.5) | copy-done | bytes 472
  9.7 0.0 copy-start.6
  9.7 0.7 %copy-done.6 = s32[4]{0:T(128)S(1)} copy-done((s32[4]{0:T(128)S(1)}, s32[4]{0:T(128)}, u32[]{:S(2)}) %copy-start.6) | copy-done | bytes 40
  10.3 0.0 copy-start.7
  10.3 0.7 %copy-done.7 = s32[4]{0:T(128)S(1)} copy-done((s32[4]{0:T(128)S(1)}, s32[4]{0:T(128)}, u32[]{:S(2)}) %copy-start.7) | copy-done | bytes 40
  11.0 3.0 %operator.1 = (bf16[448,1024]{1,0:T(8,128)(2,1)S(1)}, bf16[448,1024]{1,0:T(8,128)(2,1)S(1)}, bf16[128,512]{1,0:T(8,128)(2,1)S(1)}, bf16[128,512]{1,0:T(8,128)(2,...) custom-call(s32[1]{0:T(128)} %bitcast.4.me_ref, s32[7,16]{1,0:T(8,128)S(1)} %bitcast.15, s32[4]{0:T(128)S(1)} %copy-done.6, ...), custom_call_target="tpu_custom_call" | custom-call | flops 268435456 | bytes 16777216 | tf_op jit(solution)/shard_map/operator/pallas_call | solution.py:275
  14.0 0.0 copy-start.3
  14.0 0.0 copy-start.4
  14.1 7.8 %all-to-all-done = f32[8,16,1024]{2,0,1:T(8,128)S(1)} async-done(((f32[8,16,1024]{2,0,1:T(8,128)}), f32[8,16,1024]{2,0,1:T(8,128)S(1)}, u32[]{:S(2)}, u32[]{:S(2)}) %all-to-all-start) | async-done | bytes 524320 | tf_op jit(solution)/shard_map/all_to_all | solution.py:272
  21.9 0.5 send_0.1
  22.3 0.1 collective-permute-start
  22.4 1.6 %collective-permute-start.1 = (f32[128,256]{1,0:T(8,128)S(1)}, f32[128,256]{1,0:T(8,128)S(1)}, u32[]{:S(2)}, u32[]{:S(2)}) collective-permute-start(f32[128,256]{1,0:T(8,128)S(1)} %get-tuple-element.36), channel_id=1, source_target_pairs={{1,2},{2,1},{3,4},{4,3},{5,6},{6,5},{7,8},{8,7},{9,10},{10,9},{11,... | collective-permute-start | bytes 393224 | tf_op jit(solution)/shard_map/ppermute | solution.py:270
  24.0 2.6 %own_1.1 = (f32[128,1024]{1,0:T(8,128)S(1)}, f32[128,512]{1,0:T(8,128)S(1)}, bf16[1536,1024]{1,0:T(8,128)(2,1)S(1)}, bf16[1536,1024]{1,0:T(8,128)(2,1)S(1)}, bf1...) custom-call(f32[128,1024]{1,0:T(8,128)S(1)} %bitcast.11, bf16[448,1024]{1,0:T(8,128)(2,1)S(1)} %get-tuple-element.27.blocks_high, ...), custom_call_target="tpu_custom_call" | custom-call | flops 268435456 | bytes 4194304 | tf_op jit(solution)/shard_map/own_1/pallas_call | solution.py:294
  26.6 0.0 collective-permute-done.from_inner
  26.6 0.8 %collective-permute-done.1.from_outer = f32[128,256]{1,0:T(8,128)S(1)} collective-permute-done((f32[128,256]{1,0:T(8,128)S(1)}, f32[128,256]{1,0:T(8,128)S(1)}, u32[]{:S(2)}, u32[]{:S(2)}) %collective-permute-start.1) | collective-permute-done | bytes 131104 | tf_op jit(solution)/shard_map/ppermute | solution.py:270
  27.4 0.4 send_1.1
  27.8 0.2 collective-permute-start.2
  28.0 1.5 %collective-permute-start.3 = (f32[128,256]{1,0:T(8,128)S(1)}, f32[128,256]{1,0:T(8,128)S(1)}, u32[]{:S(2)}, u32[]{:S(2)}) collective-permute-start(f32[128,256]{1,0:T(8,128)S(1)} %get-tuple-element.44), channel_id=1, source_target_pairs={{1,2},{2,1},{3,4},{4,3},{5,6},{6,5},{7,8},{8,7},{9,10},{10,9},{11,... | collective-permute-start | bytes 393224 | tf_op jit(solution)/shard_map/ppermute | solution.py:270
  29.5 0.0 copy-done.3
  29.5 0.0 copy-done.4
  29.5 0.0 copy-start.1
  29.5 0.0 copy-start.2
  29.5 2.1 %own_2.1 = (f32[128,1024]{1,0:T(8,128)S(1)}, f32[128,512]{1,0:T(8,128)S(1)}, f32[128,1024]{1,0:T(8,128)S(1)}) custom-call(f32[128,1024]{1,0:T(8,128)S(1)} %bitcast.12, f32[128,1024]{1,0:T(8,128)S(1)} %get-tuple-element.34.part_ref, f32[128,256]{1,0:T(8,128)S(1)} %collective-permute-done.from_inner, f32[128,256]{1,0:T(8,128)S(1)} %collective-permute-done.1.from_outer, ...), custom_call_target="tpu_custom_call" | custom-call | flops 268435456 | bytes 4194304 | tf_op jit(solution)/shard_map/own_2/pallas_call | solution.py:303
  31.6 0.0 collective-permute-done.2.from_inner
  31.6 1.3 %collective-permute-done.3.from_outer = f32[128,256]{1,0:T(8,128)S(1)} collective-permute-done((f32[128,256]{1,0:T(8,128)S(1)}, f32[128,256]{1,0:T(8,128)S(1)}, u32[]{:S(2)}, u32[]{:S(2)}) %collective-permute-start.3) | collective-permute-done | bytes 131104 | tf_op jit(solution)/shard_map/ppermute | solution.py:270
  33.0 0.0 copy-done.1
  33.0 0.5 send_2.1
  33.5 0.2 collective-permute-start.4
  33.7 1.5 %collective-permute-start.5 = (f32[128,256]{1,0:T(8,128)S(1)}, f32[128,256]{1,0:T(8,128)S(1)}, u32[]{:S(2)}, u32[]{:S(2)}) collective-permute-start(f32[128,256]{1,0:T(8,128)S(1)} %get-tuple-element.48), channel_id=1, source_target_pairs={{1,2},{2,1},{3,4},{4,3},{5,6},{6,5},{7,8},{8,7},{9,10},{10,9},{11,... | collective-permute-start | bytes 393224 | tf_op jit(solution)/shard_map/ppermute | solution.py:270
  35.2 0.0 copy-done.2
  35.2 1.9 %own_3.1.part_ref = f32[128,1024]{1,0:T(8,128)S(1)} custom-call(f32[128,1024]{1,0:T(8,128)S(1)} %get-tuple-element.39.part_ref, f32[128,256]{1,0:T(8,128)S(1)} %collective-permute-done.2.from_inner, f32[128,256]{1,0:T(8,128)S(1)} %collective-permute-done.3.from_outer, f32[128,1024]{1,0:T(8,128)S(1)} %get-tuple-element.45.total_ref, ...), custom_call_target="tpu_custom_call" | custom-call | flops 268435456 | bytes 4194304 | tf_op jit(solution)/shard_map/own_3/pallas_call | solution.py:311
  37.0 0.0 collective-permute-done.4.from_inner
  37.0 1.6 %collective-permute-done.5.from_outer = f32[128,256]{1,0:T(8,128)S(1)} collective-permute-done((f32[128,256]{1,0:T(8,128)S(1)}, f32[128,256]{1,0:T(8,128)S(1)}, u32[]{:S(2)}, u32[]{:S(2)}) %collective-permute-start.5) | collective-permute-done | bytes 131104 | tf_op jit(solution)/shard_map/ppermute | solution.py:270
  38.6 0.3 close.1
  39.0 18.2 %all_to_all.38 = f32[16,8,1024]{2,1,0:T(8,128)S(1)} all-to-all(f32[16,8,1024]{2,1,0:T(8,128)S(1)} %bitcast.13), channel_id=1, replica_groups={{5,8,12,4,9,10,6,7,14,1,15,2,11,13,3,0},{21,24,28,20,25,26,22,23,30,17,..., dimensions={0} | all-to-all | bytes 1048576 | tf_op jit(solution)/shard_map/all_to_all | solution.py:313
  57.2 0.9 %store.1 = f32[8,16384]{1,0:T(8,128)} custom-call(f32[8,16384]{1,0:T(8,128)S(1)} %bitcast.14), custom_call_target="tpu_custom_call" | custom-call | flops 268435456 | bytes 4194304 | tf_op jit(solution)/shard_map/store/pallas_call | solution.py:316
Async XLA Ops:
  0.0 21.9 %all-to-all-start = ((f32[8,16,1024]{2,0,1:T(8,128)}), f32[8,16,1024]{2,0,1:T(8,128)S(1)}, u32[]{:S(2)}, u32[]{:S(2)}) async-start(f32[8,16,1024]{2,0,1:T(8,128)} %bitcast.16), calls=%async_computation | async-start | bytes 1048576 | tf_op jit(solution)/shard_map/all_to_all | solution.py:272
  7.4 1.6 %copy-start = (f32[16,64,448]{2,1,0:T(8,128)S(1)}, f32[16,64,448]{2,1,0:T(8,128)}, u32[]{:S(2)}) copy-start(f32[16,64,448]{2,1,0:T(8,128)} %blocks_in.1) | copy-start | bytes 5505028
  9.0 0.7 %copy-start.5 = (s32[16,7]{0,1:T(8,128)S(1)}, s32[16,7]{0,1:T(8,128)}, u32[]{:S(2)}) copy-start(s32[16,7]{0,1:T(8,128)} %param.11) | copy-start | bytes 1348
  9.7 0.7 %copy-start.6 = (s32[4]{0:T(128)S(1)}, s32[4]{0:T(128)}, u32[]{:S(2)}) copy-start(s32[4]{0:T(128)} %up_ref.1) | copy-start | bytes 52
  10.3 0.7 %copy-start.7 = (s32[4]{0:T(128)S(1)}, s32[4]{0:T(128)}, u32[]{:S(2)}) copy-start(s32[4]{0:T(128)} %down_ref.1) | copy-start | bytes 52
  14.0 15.5 %copy-start.3 = (bf16[256,128]{1,0:T(8,128)(2,1)S(1)}, bf16[256,128]{1,0:T(8,128)(2,1)}, u32[]{:S(2)}) copy-start(bf16[256,128]{1,0:T(8,128)(2,1)} %constant.30.table1_ref) | copy-start | bytes 196612
  14.0 15.4 %copy-start.4 = (bf16[256,128]{1,0:T(8,128)(2,1)S(1)}, bf16[256,128]{1,0:T(8,128)(2,1)}, u32[]{:S(2)}) copy-start(bf16[256,128]{1,0:T(8,128)(2,1)} %constant.25.table0_ref) | copy-start | bytes 196612
  22.3 4.3 %collective-permute-start = (f32[128,256]{1,0:T(8,128)S(1)}, f32[128,256]{1,0:T(8,128)S(1)}, u32[]{:S(2)}, u32[]{:S(2)}) collective-permute-start(f32[128,256]{1,0:T(8,128)S(1)} %get-tuple-element.35), channel_id=1, source_target_pairs={{0,1},{1,0},{2,3},{3,2},{4,5},{5,4},{6,7},{7,6},{8,9},{9,8},{10,11... | collective-permute-start | bytes 393224 | tf_op jit(solution)/shard_map/ppermute | solution.py:270
  22.4 5.0 %collective-permute-start.1 = (f32[128,256]{1,0:T(8,128)S(1)}, f32[128,256]{1,0:T(8,128)S(1)}, u32[]{:S(2)}, u32[]{:S(2)}) collective-permute-start(f32[128,256]{1,0:T(8,128)S(1)} %get-tuple-element.36), channel_id=1, source_target_pairs={{1,2},{2,1},{3,4},{4,3},{5,6},{6,5},{7,8},{8,7},{9,10},{10,9},{11,... | collective-permute-start | bytes 393224 | tf_op jit(solution)/shard_map/ppermute | solution.py:270
  27.8 3.8 %collective-permute-start.2 = (f32[128,256]{1,0:T(8,128)S(1)}, f32[128,256]{1,0:T(8,128)S(1)}, u32[]{:S(2)}, u32[]{:S(2)}) collective-permute-start(f32[128,256]{1,0:T(8,128)S(1)} %get-tuple-element.43), channel_id=1, source_target_pairs={{0,1},{1,0},{2,3},{3,2},{4,5},{5,4},{6,7},{7,6},{8,9},{9,8},{10,11... | collective-permute-start | bytes 393224 | tf_op jit(solution)/shard_map/ppermute | solution.py:270
  28.0 5.0 %collective-permute-start.3 = (f32[128,256]{1,0:T(8,128)S(1)}, f32[128,256]{1,0:T(8,128)S(1)}, u32[]{:S(2)}, u32[]{:S(2)}) collective-permute-start(f32[128,256]{1,0:T(8,128)S(1)} %get-tuple-element.44), channel_id=1, source_target_pairs={{1,2},{2,1},{3,4},{4,3},{5,6},{6,5},{7,8},{8,7},{9,10},{10,9},{11,... | collective-permute-start | bytes 393224 | tf_op jit(solution)/shard_map/ppermute | solution.py:270
  29.5 3.5 %copy-start.1 = (bf16[256,128]{1,0:T(8,128)(2,1)S(1)}, bf16[256,128]{1,0:T(8,128)(2,1)}, u32[]{:S(2)}) copy-start(bf16[256,128]{1,0:T(8,128)(2,1)} %constant.40.table3_ref.table_ref) | copy-start | bytes 196612
  29.5 5.7 %copy-start.2 = (bf16[256,128]{1,0:T(8,128)(2,1)S(1)}, bf16[256,128]{1,0:T(8,128)(2,1)}, u32[]{:S(2)}) copy-start(bf16[256,128]{1,0:T(8,128)(2,1)} %constant.35.table2_ref) | copy-start | bytes 196612
  33.5 3.5 %collective-permute-start.4 = (f32[128,256]{1,0:T(8,128)S(1)}, f32[128,256]{1,0:T(8,128)S(1)}, u32[]{:S(2)}, u32[]{:S(2)}) collective-permute-start(f32[128,256]{1,0:T(8,128)S(1)} %get-tuple-element.47), channel_id=1, source_target_pairs={{0,1},{1,0},{2,3},{3,2},{4,5},{5,4},{6,7},{7,6},{8,9},{9,8},{10,11... | collective-permute-start | bytes 393224 | tf_op jit(solution)/shard_map/ppermute | solution.py:270
  33.7 5.0 %collective-permute-start.5 = (f32[128,256]{1,0:T(8,128)S(1)}, f32[128,256]{1,0:T(8,128)S(1)}, u32[]{:S(2)}, u32[]{:S(2)}) collective-permute-start(f32[128,256]{1,0:T(8,128)S(1)} %get-tuple-element.48), channel_id=1, source_target_pairs={{1,2},{2,1},{3,4},{4,3},{5,6},{6,5},{7,8},{8,7},{9,10},{10,9},{11,... | collective-permute-start | bytes 393224 | tf_op jit(solution)/shard_map/ppermute | solution.py:270

commit v5 on v4

--- a/solution.py
+++ b/solution.py
@@ -61,7 +61,7 @@
 
 def build_kernel(
     count, me_ref, columns_ref, up_ref, down_ref, blocks_in,
-    high_ref, low_ref, sent_high_ref, sent_low_ref, place_ref, table_ref, blocks_ref, block_sems,
+    high_ref, low_ref, pick_ref, table_ref, blocks_ref, block_sems,
 ):
     rows, size, _ = blocks_ref.shape
     halo = up_ref.shape[0]
@@ -104,19 +104,11 @@
             high, low = halves(part[slot])
             high_ref[slot * size : (slot + 1) * size, lanes] = high
             low_ref[slot * size : (slot + 1) * size, lanes] = low
-    wide = lax.broadcasted_iota(jnp.int32, (2 * size, 2 * size), 1)
+    down = lax.broadcasted_iota(jnp.int32, (rows * size, 2 * size), 0)
+    across = lax.broadcasted_iota(jnp.int32, (rows * size, 2 * size), 1)
     for pair in range(halo):
-        lanes = slice(pair * 2 * size, (pair + 1) * 2 * size)
-        for whole_ref, few_ref in ((high_ref, sent_high_ref), (low_ref, sent_low_ref)):
-            parts = []
-            for half in range(2):
-                row = sent[2 * pair + half]
-                at = pl.ds(pl.multiple_of((row // 2) * 2 * size, 2 * size), 2 * size)
-                tile = whole_ref[size : 3 * size, at].astype(jnp.float32)
-                parts.append(jnp.where(lax.rem(row, 2) == half, tile, pltpu.roll(tile, size, 1)))
-            few_ref[:, lanes] = jnp.where(wide < size, parts[0], parts[1]).astype(jnp.bfloat16)
-        across = lax.broadcasted_iota(jnp.int32, (place_ref.shape[0], 2 * size), 1)
-        place_ref[:, lanes] = jnp.where(across < size, sent[2 * pair], sent[2 * pair + 1] - 1) * size + across
+        place = jnp.where(across < size, sent[2 * pair], sent[2 * pair + 1] - 1) * size + across
+        pick_ref[:, pair * 2 * size : (pair + 1) * 2 * size] = jnp.where(down == place, 1.0, 0.0).astype(jnp.bfloat16)
 
 
 def store_sent(value, inner_ref, outer_ref):
@@ -132,14 +124,12 @@
     return both[:rows] + both[rows:]
 
 
-def first_kernel(value_ref, place_ref, inner_ref, outer_ref, pick_ref):
-    down = lax.broadcasted_iota(jnp.int32, pick_ref.shape, 0)
-    pick_ref[...] = jnp.where(down == place_ref[0:1, :], 1.0, 0.0).astype(jnp.bfloat16)
+def first_kernel(value_ref, pick_ref, inner_ref, outer_ref):
     store_sent(picked(value_ref[...], pick_ref), inner_ref, outer_ref)
 
 
 def own_first_kernel(
-    value_ref, blocks_high, blocks_low, sent_high, sent_low, pick_ref, table_in,
+    value_ref, blocks_high, blocks_low, pick_ref, table_in,
     out_ref, sent_ref, high_ref, low_ref, halo_high, halo_low, table_ref, sem,
 ):
     times, own = value_ref.shape
@@ -156,13 +146,16 @@
             lanes = slice(row * size, (row + 1) * size)
             high_ref[at, lanes] = blocks_high[slot * size : (slot + 1) * size, lanes]
             low_ref[at, lanes] = blocks_low[slot * size : (slot + 1) * size, lanes]
-    for index in range(sent_high.shape[1] // size):
+    for index in range(sent_ref.shape[1] // size):
         row = table_ref[SLOTS, index]
-        lanes = slice(index * size, (index + 1) * size)
+        half = index % 2
+        pair = pl.ds(pl.multiple_of((row // 2) * 2 * size, 2 * size), 2 * size)
         for slot in (1, 2):
             at = pl.ds(pl.multiple_of((table_ref[slot, row] - rows) * size, size), size)
-            halo_high[at, lanes] = sent_high[(slot - 1) * size : slot * size, lanes]
-            halo_low[at, lanes] = sent_low[(slot - 1) * size : slot * size, lanes]
+            for whole_ref, few_ref in ((blocks_high, halo_high), (blocks_low, halo_low)):
+                tile = whole_ref[slot * size : (slot + 1) * size, pair].astype(jnp.float32)
+                tile = jnp.where(lax.rem(row, 2) == half, tile, pltpu.roll(tile, size, 1)).astype(jnp.bfloat16)
+                few_ref[at, index * size : (index + 1) * size] = tile[:, half * size : (half + 1) * size]
     out_ref[...] = mm_split(value_ref[...], high_ref[:own], low_ref[:own])
     sent_ref[...] = picked(out_ref[...], pick_ref)
 
@@ -182,8 +175,8 @@
     store_sent(value, inner_ref, outer_ref)
 
 
-def send_last_kernel(part_ref, from_inner, from_outer, halo_high, halo_low, table_ref, inner_ref, outer_ref):
-    value = part_ref[...] + halo_product(from_inner, from_outer, halo_high[...], halo_low[...])
+def send_last_kernel(part_ref, from_inner, from_outer, halo_high, table_ref, inner_ref, outer_ref):
+    value = part_ref[...] + halo_once(from_inner, from_outer, halo_high[...])
     table = table_ref[: value.shape[0]]
     store_sent(mm(table, value.astype(jnp.bfloat16)), inner_ref, outer_ref)
 
@@ -272,30 +265,29 @@
     start = lax.all_to_all(source, "space", split_axis=1, concat_axis=0, tiled=True)
     side = own + 2 * width
     dma = pltpu.SemaphoreType.DMA
-    *blocked, place, table = call(
+    *blocked, pick, table = call(
         functools.partial(build_kernel, count),
         (
             *[bf16(SLOTS * BS, own)] * 2,
-            *[bf16(2 * BS, 2 * width)] * 2,
-            jax.ShapeDtypeStruct((8, 2 * width), jnp.int32),
+            bf16(own, 2 * width),
             jax.ShapeDtypeStruct((SLOTS + 1, rows), jnp.int32),
         ),
         "operator",
         [SMEM] * 4 + [ANY],
-        (VMEM,) * 5 + (SMEM,),
+        (VMEM,) * 3 + (SMEM,),
         scratch=[pltpu.VMEM(blocks.shape, jnp.float32), dma((rows // 2,))],
         moved=16 << 20,
     )(me, columns.T, rows_up, rows_down, blocks)
     sent = (f32(times, width), f32(times, width))
     value, ahead = f32(times, own), f32(times, 2 * width)
 
-    inner, outer, pick = call(first_kernel, (*sent, bf16(own, 2 * width)), "send_0", [VMEM] * 2)(start, place)
+    inner, outer = call(first_kernel, sent, "send_0", [VMEM] * 2)(start, pick)
     inner, outer = swap(inner, outer)
     part, part_sent, high, low, *halo_parts = call(
         own_first_kernel,
         (value, ahead, *[bf16(side, own)] * 2, *[bf16(2 * width, 2 * width)] * 2),
         "own_1",
-        [VMEM] * 6 + [ANY],
+        [VMEM] * 4 + [ANY],
         scratch=[pltpu.SMEM((SLOTS + 1, rows), jnp.int32), dma],
     )(start, *blocked, pick, table)
     next_inner, next_outer = call(send_kernel, sent, "send_1", [VMEM] * 5)(part_sent, inner, outer, *halo_parts)
@@ -304,8 +296,8 @@
         start, part, inner, outer, high, low, pick, tables[0], tables[1]
     )
     inner, outer = next_inner, next_outer
-    next_inner, next_outer = call(send_last_kernel, sent, "send_2", [VMEM] * 6)(
-        part_sent, inner, outer, *halo_parts, tables[3]
+    next_inner, next_outer = call(send_last_kernel, sent, "send_2", [VMEM] * 5)(
+        part_sent, inner, outer, halo_parts[0], tables[3]
     )
     next_inner, next_outer = swap(next_inner, next_outer)
     part = call(own_third_kernel, value, "own_3", [VMEM] * 8)(part, inner, outer, total, high, low, tables[2], tables[3])

time: 58.4 us -> 58.3 us (level)
  transfers between devices with their start and end apart: 7 -> 7, of which waited for: 4 -> 4; matrix products, arithmetic and copies ran while one was open for 0% -> 0% of each run, Pallas kernels for 17% -> 16%
where the time goes in v5:
time: 58.3 us; the launch traced here: 57.9 us
  blocking collectives  18.2 us (31%)
  starting transfers between devices  12.4 us (21%)
  Pallas kernels  11.9 us (20%)
  waiting for transfers between devices  11.7 us (20%)
  local copies, waits for them, and re-layouts  3.6 us (6%)
    all_to_all x1, blocking collectives, per_device(): lax.all_to_all(timed, 'space', split_axis=0, concat_axis=1, tiled=True, a...  18.2 us
    all_to_all x1, waiting for transfers between devices, per_device(): lax.all_to_all(source, 'space', split_axis=1, concat_axis=0, tiled=True)  7.96 us
    all_to_all x1, starting transfers between devices, per_device(): lax.all_to_all(source, 'space', split_axis=1, concat_axis=0, tiled=True)  7.38 us
    ppermute x3, starting transfers between devices, swap(): lax.ppermute(outer, ('group', 'space'), outer_pairs)  4.53 us
    ppermute x3, waiting for transfers between devices, swap(): lax.ppermute(outer, ('group', 'space'), outer_pairs)  3.74 us
    unnamed x16, local copies, waits for them, and re-layouts  3.6 us
    pallas_call x1, Pallas kernels, per_device(): call(functools.partial(build_kernel, count), (*[bf16(SLOTS * BS, own)] *...  2.9 us
    pallas_call x1, Pallas kernels, per_device(): call(own_first_kernel, (value, ahead, *[bf16(side, own)] * 2, *[bf16(2 *...  2.65 us
  transfers between devices with their start and end apart: 7, of which 4 were waited for; matrix products, arithmetic and copies ran while one was open for 0% of the time, Pallas kernels for 16%

profile of v5, /device:TPU:0, one launch (start us, length us, event | category | flops | bytes accessed | tf_op | source)
XLA Modules:
  0.0 57.9 jit_solution(13401585193017286545)
XLA Ops:
  0.0 7.4 %all-to-all-start = ((f32[8,16,1024]{2,0,1:T(8,128)}), f32[8,16,1024]{2,0,1:T(8,128)S(1)}, u32[]{:S(2)}, u32[]{:S(2)}) async-start(f32[8,16,1024]{2,0,1:T(8,128)} %bitcast.16), calls=%async_computation | async-start | bytes 1048576 | tf_op jit(solution)/shard_map/all_to_all | solution.py:265
  7.4 0.0 copy-start
  7.4 1.6 %copy-done = f32[16,64,448]{2,1,0:T(8,128)S(1)} copy-done((f32[16,64,448]{2,1,0:T(8,128)S(1)}, f32[16,64,448]{2,1,0:T(8,128)}, u32[]{:S(2)}) %copy-start) | copy-done | bytes 1835032
  9.0 0.0 copy-start.5
  9.0 0.7 %copy-done.5 = s32[16,7]{0,1:T(8,128)S(1)} copy-done((s32[16,7]{0,1:T(8,128)S(1)}, s32[16,7]{0,1:T(8,128)}, u32[]{:S(2)}) %copy-start.5) | copy-done | bytes 472
  9.7 0.0 copy-start.6
  9.7 0.7 %copy-done.6 = s32[4]{0:T(128)S(1)} copy-done((s32[4]{0:T(128)S(1)}, s32[4]{0:T(128)}, u32[]{:S(2)}) %copy-start.6) | copy-done | bytes 40
  10.3 0.0 copy-start.7
  10.3 0.7 %copy-done.7 = s32[4]{0:T(128)S(1)} copy-done((s32[4]{0:T(128)S(1)}, s32[4]{0:T(128)}, u32[]{:S(2)}) %copy-start.7) | copy-done | bytes 40
  11.0 2.9 %operator.1 = (bf16[448,1024]{1,0:T(8,128)(2,1)S(1)}, bf16[448,1024]{1,0:T(8,128)(2,1)S(1)}, bf16[1024,512]{1,0:T(8,128)(2,1)S(1)}, s32[8,16]{1,0:T(8,128)S(1)}) custom-call(s32[1]{0:T(128)} %bitcast.4.me_ref, s32[7,16]{1,0:T(8,128)S(1)} %bitcast.15, s32[4]{0:T(128)S(1)} %copy-done.6, s32[4]{0:T(128)S(1)} %copy-done.7, f32[16,64,448]{2,1,0:T(8,128)S(1)} %copy-done), custom_call_target="tpu_custom_call" | custom-call | flops 268435456 | bytes 16777216 | tf_op jit(solution)/shard_map/operator/pallas_call | solution.py:268
  13.9 8.0 %all-to-all-done = f32[8,16,1024]{2,0,1:T(8,128)S(1)} async-done(((f32[8,16,1024]{2,0,1:T(8,128)}), f32[8,16,1024]{2,0,1:T(8,128)S(1)}, u32[]{:S(2)}, u32[]{:S(2)}) %all-to-all-start) | async-done | bytes 524320 | tf_op jit(solution)/shard_map/all_to_all | solution.py:265
  21.9 0.0 copy-start.3
  21.9 0.0 copy-start.4
  21.9 0.4 send_0.1
  22.3 0.1 collective-permute-start
  22.4 1.6 %collective-permute-start.1 = (f32[128,256]{1,0:T(8,128)S(1)}, f32[128,256]{1,0:T(8,128)S(1)}, u32[]{:S(2)}, u32[]{:S(2)}) collective-permute-start(f32[128,256]{1,0:T(8,128)S(1)} %get-tuple-element.30), channel_id=1, source_target_pairs={{1,2},{2,1},{3,4},{4,3},{5,6},{6,5},{7,8},{8,7},{9,10},{10,9},{11,... | collective-permute-start | bytes 393224 | tf_op jit(solution)/shard_map/ppermute | solution.py:263
  23.9 2.6 %own_1.1 = (f32[128,1024]{1,0:T(8,128)S(1)}, f32[128,512]{1,0:T(8,128)S(1)}, bf16[1536,1024]{1,0:T(8,128)(2,1)S(1)}, bf16[1536,1024]{1,0:T(8,128)(2,1)S(1)}, bf1...) custom-call(f32[128,1024]{1,0:T(8,128)S(1)} %bitcast.11, bf16[448,1024]{1,0:T(8,128)(2,1)S(1)} %get-tuple-element.24.blocks_high, ...), custom_call_target="tpu_custom_call" | custom-call | flops 268435456 | bytes 4194304 | tf_op jit(solution)/shard_map/own_1/pallas_call | solution.py:286
  26.6 0.0 collective-permute-done.from_inner
  26.6 0.8 %collective-permute-done.1.from_outer = f32[128,256]{1,0:T(8,128)S(1)} collective-permute-done((f32[128,256]{1,0:T(8,128)S(1)}, f32[128,256]{1,0:T(8,128)S(1)}, u32[]{:S(2)}, u32[]{:S(2)}) %collective-permute-start.1) | collective-permute-done | bytes 131104 | tf_op jit(solution)/shard_map/ppermute | solution.py:263
  27.4 0.4 send_1.1
  27.8 0.2 collective-permute-start.2
  28.0 1.5 %collective-permute-start.3 = (f32[128,256]{1,0:T(8,128)S(1)}, f32[128,256]{1,0:T(8,128)S(1)}, u32[]{:S(2)}, u32[]{:S(2)}) collective-permute-start(f32[128,256]{1,0:T(8,128)S(1)} %get-tuple-element.38), channel_id=1, source_target_pairs={{1,2},{2,1},{3,4},{4,3},{5,6},{6,5},{7,8},{8,7},{9,10},{10,9},{11,... | collective-permute-start | bytes 393224 | tf_op jit(solution)/shard_map/ppermute | solution.py:263
  29.5 0.0 copy-done.3
  29.5 0.0 copy-done.4
  29.5 0.0 copy-start.1
  29.5 0.0 copy-start.2
  29.5 2.1 %own_2.1 = (f32[128,1024]{1,0:T(8,128)S(1)}, f32[128,512]{1,0:T(8,128)S(1)}, f32[128,1024]{1,0:T(8,128)S(1)}) custom-call(f32[128,1024]{1,0:T(8,128)S(1)} %bitcast.12, f32[128,1024]{1,0:T(8,128)S(1)} %get-tuple-element.28.part_ref, f32[128,256]{1,0:T(8,128)S(1)} %collective-permute-done.from_inner, f32[128,256]{1,0:T(8,128)S(1)} %collective-permute-done.1.from_outer, ...), custom_call_target="tpu_custom_call" | custom-call | flops 268435456 | bytes 4194304 | tf_op jit(solution)/shard_map/own_2/pallas_call | solution.py:295
  31.6 0.0 collective-permute-done.2.from_inner
  31.6 1.3 %collective-permute-done.3.from_outer = f32[128,256]{1,0:T(8,128)S(1)} collective-permute-done((f32[128,256]{1,0:T(8,128)S(1)}, f32[128,256]{1,0:T(8,128)S(1)}, u32[]{:S(2)}, u32[]{:S(2)}) %collective-permute-start.3) | collective-permute-done | bytes 131104 | tf_op jit(solution)/shard_map/ppermute | solution.py:263
  32.9 0.0 copy-done.1
  32.9 0.4 send_2.1
  33.3 0.2 collective-permute-start.4
  33.5 1.5 %collective-permute-start.5 = (f32[128,256]{1,0:T(8,128)S(1)}, f32[128,256]{1,0:T(8,128)S(1)}, u32[]{:S(2)}, u32[]{:S(2)}) collective-permute-start(f32[128,256]{1,0:T(8,128)S(1)} %get-tuple-element.42), channel_id=1, source_target_pairs={{1,2},{2,1},{3,4},{4,3},{5,6},{6,5},{7,8},{8,7},{9,10},{10,9},{11,... | collective-permute-start | bytes 393224 | tf_op jit(solution)/shard_map/ppermute | solution.py:263
  35.0 0.0 copy-done.2
  35.0 1.9 %own_3.1.part_ref = f32[128,1024]{1,0:T(8,128)S(1)} custom-call(f32[128,1024]{1,0:T(8,128)S(1)} %get-tuple-element.33.part_ref, f32[128,256]{1,0:T(8,128)S(1)} %collective-permute-done.2.from_inner, f32[128,256]{1,0:T(8,128)S(1)} %collective-permute-done.3.from_outer, f32[128,1024]{1,0:T(8,128)S(1)} %get-tuple-element.39.total_ref, ...), custom_call_target="tpu_custom_call" | custom-call | flops 268435456 | bytes 4194304 | tf_op jit(solution)/shard_map/own_3/pallas_call | solution.py:303
  36.9 0.0 collective-permute-done.4.from_inner
  36.9 1.6 %collective-permute-done.5.from_outer = f32[128,256]{1,0:T(8,128)S(1)} collective-permute-done((f32[128,256]{1,0:T(8,128)S(1)}, f32[128,256]{1,0:T(8,128)S(1)}, u32[]{:S(2)}, u32[]{:S(2)}) %collective-permute-start.5) | collective-permute-done | bytes 131104 | tf_op jit(solution)/shard_map/ppermute | solution.py:263
  38.5 0.3 close.1
  38.8 18.2 %all_to_all.38 = f32[16,8,1024]{2,1,0:T(8,128)S(1)} all-to-all(f32[16,8,1024]{2,1,0:T(8,128)S(1)} %bitcast.13), channel_id=1, replica_groups={{5,8,12,4,9,10,6,7,14,1,15,2,11,13,3,0},{21,24,28,20,25,26,22,23,30,17,..., dimensions={0} | all-to-all | bytes 1048576 | tf_op jit(solution)/shard_map/all_to_all | solution.py:305
  57.0 0.9 %store.1 = f32[8,16384]{1,0:T(8,128)} custom-call(f32[8,16384]{1,0:T(8,128)S(1)} %bitcast.14), custom_call_target="tpu_custom_call" | custom-call | flops 268435456 | bytes 4194304 | tf_op jit(solution)/shard_map/store/pallas_call | solution.py:308
Async XLA Ops:
  0.0 21.9 %all-to-all-start = ((f32[8,16,1024]{2,0,1:T(8,128)}), f32[8,16,1024]{2,0,1:T(8,128)S(1)}, u32[]{:S(2)}, u32[]{:S(2)}) async-start(f32[8,16,1024]{2,0,1:T(8,128)} %bitcast.16), calls=%async_computation | async-start | bytes 1048576 | tf_op jit(solution)/shard_map/all_to_all | solution.py:265
  7.4 1.6 %copy-start = (f32[16,64,448]{2,1,0:T(8,128)S(1)}, f32[16,64,448]{2,1,0:T(8,128)}, u32[]{:S(2)}) copy-start(f32[16,64,448]{2,1,0:T(8,128)} %blocks_in.1) | copy-start | bytes 5505028
  9.0 0.7 %copy-start.5 = (s32[16,7]{0,1:T(8,128)S(1)}, s32[16,7]{0,1:T(8,128)}, u32[]{:S(2)}) copy-start(s32[16,7]{0,1:T(8,128)} %param.11) | copy-start | bytes 1348
  9.7 0.7 %copy-start.6 = (s32[4]{0:T(128)S(1)}, s32[4]{0:T(128)}, u32[]{:S(2)}) copy-start(s32[4]{0:T(128)} %up_ref.1) | copy-start | bytes 52
  10.3 0.7 %copy-start.7 = (s32[4]{0:T(128)S(1)}, s32[4]{0:T(128)}, u32[]{:S(2)}) copy-start(s32[4]{0:T(128)} %down_ref.1) | copy-start | bytes 52
  21.9 7.6 %copy-start.3 = (bf16[256,128]{1,0:T(8,128)(2,1)S(1)}, bf16[256,128]{1,0:T(8,128)(2,1)}, u32[]{:S(2)}) copy-start(bf16[256,128]{1,0:T(8,128)(2,1)} %constant.25.table0_ref) | copy-start | bytes 196612
  21.9 7.6 %copy-start.4 = (bf16[256,128]{1,0:T(8,128)(2,1)S(1)}, bf16[256,128]{1,0:T(8,128)(2,1)}, u32[]{:S(2)}) copy-start(bf16[256,128]{1,0:T(8,128)(2,1)} %constant.30.table1_ref) | copy-start | bytes 196612
  22.3 4.3 %collective-permute-start = (f32[128,256]{1,0:T(8,128)S(1)}, f32[128,256]{1,0:T(8,128)S(1)}, u32[]{:S(2)}, u32[]{:S(2)}) collective-permute-start(f32[128,256]{1,0:T(8,128)S(1)} %get-tuple-element.29), channel_id=1, source_target_pairs={{0,1},{1,0},{2,3},{3,2},{4,5},{5,4},{6,7},{7,6},{8,9},{9,8},{10,11... | collective-permute-start | bytes 393224 | tf_op jit(solution)/shard_map/ppermute | solution.py:263
  22.4 5.0 %collective-permute-start.1 = (f32[128,256]{1,0:T(8,128)S(1)}, f32[128,256]{1,0:T(8,128)S(1)}, u32[]{:S(2)}, u32[]{:S(2)}) collective-permute-start(f32[128,256]{1,0:T(8,128)S(1)} %get-tuple-element.30), channel_id=1, source_target_pairs={{1,2},{2,1},{3,4},{4,3},{5,6},{6,5},{7,8},{8,7},{9,10},{10,9},{11,... | collective-permute-start | bytes 393224 | tf_op jit(solution)/shard_map/ppermute | solution.py:263
  27.8 3.8 %collective-permute-start.2 = (f32[128,256]{1,0:T(8,128)S(1)}, f32[128,256]{1,0:T(8,128)S(1)}, u32[]{:S(2)}, u32[]{:S(2)}) collective-permute-start(f32[128,256]{1,0:T(8,128)S(1)} %get-tuple-element.37), channel_id=1, source_target_pairs={{0,1},{1,0},{2,3},{3,2},{4,5},{5,4},{6,7},{7,6},{8,9},{9,8},{10,11... | collective-permute-start | bytes 393224 | tf_op jit(solution)/shard_map/ppermute | solution.py:263
  28.0 5.0 %collective-permute-start.3 = (f32[128,256]{1,0:T(8,128)S(1)}, f32[128,256]{1,0:T(8,128)S(1)}, u32[]{:S(2)}, u32[]{:S(2)}) collective-permute-start(f32[128,256]{1,0:T(8,128)S(1)} %get-tuple-element.38), channel_id=1, source_target_pairs={{1,2},{2,1},{3,4},{4,3},{5,6},{6,5},{7,8},{8,7},{9,10},{10,9},{11,... | collective-permute-start | bytes 393224 | tf_op jit(solution)/shard_map/ppermute | solution.py:263
  29.5 3.5 %copy-start.1 = (bf16[256,128]{1,0:T(8,128)(2,1)S(1)}, bf16[256,128]{1,0:T(8,128)(2,1)}, u32[]{:S(2)}) copy-start(bf16[256,128]{1,0:T(8,128)(2,1)} %constant.40.table3_ref.table_ref) | copy-start | bytes 196612
  29.5 5.5 %copy-start.2 = (bf16[256,128]{1,0:T(8,128)(2,1)S(1)}, bf16[256,128]{1,0:T(8,128)(2,1)}, u32[]{:S(2)}) copy-start(bf16[256,128]{1,0:T(8,128)(2,1)} %constant.35.table2_ref) | copy-start | bytes 196612
  33.3 3.5 %collective-permute-start.4 = (f32[128,256]{1,0:T(8,128)S(1)}, f32[128,256]{1,0:T(8,128)S(1)}, u32[]{:S(2)}, u32[]{:S(2)}) collective-permute-start(f32[128,256]{1,0:T(8,128)S(1)} %get-tuple-element.41), channel_id=1, source_target_pairs={{0,1},{1,0},{2,3},{3,2},{4,5},{5,4},{6,7},{7,6},{8,9},{9,8},{10,11... | collective-permute-start | bytes 393224 | tf_op jit(solution)/shard_map/ppermute | solution.py:263
  33.5 5.0 %collective-permute-start.5 = (f32[128,256]{1,0:T(8,128)S(1)}, f32[128,256]{1,0:T(8,128)S(1)}, u32[]{:S(2)}, u32[]{:S(2)}) collective-permute-start(f32[128,256]{1,0:T(8,128)S(1)} %get-tuple-element.42), channel_id=1, source_target_pairs={{1,2},{2,1},{3,4},{4,3},{5,6},{6,5},{7,8},{8,7},{9,10},{10,9},{11,... | collective-permute-start | bytes 393224 | tf_op jit(solution)/shard_map/ppermute | solution.py:263

commit v6 on v5

--- a/solution.py
+++ b/solution.py
@@ -206,20 +206,19 @@
     out_ref[...] = part_ref[...] + halo_once(from_inner, from_outer, high_ref[own:])
 
 
-def store_kernel(order, value_ref, out_ref, sems):
+def store_kernel(order, value_ref, out_ref, sem):
     step = value_ref.shape[1] // len(order)
     copies = [
         pltpu.make_async_copy(
             value_ref.at[:, index * step : (index + 1) * step],
             out_ref.at[:, sender * step : (sender + 1) * step],
-            sems.at[index],
+            sem,
         )
         for index, sender in enumerate(order)
     ]
     for copy in copies:
         copy.start()
-    for copy in copies:
-        copy.wait()
+    pltpu.make_async_copy(value_ref, out_ref, sem).wait()
 
 
 def call(kernel, outs, name, ins, out_specs=None, scratch=(), moved=4 << 20):
@@ -311,7 +310,7 @@
         "store",
         [VMEM],
         ANY,
-        scratch=[pltpu.SemaphoreType.DMA((count,))],
+        scratch=[pltpu.SemaphoreType.DMA],
     )(field)
 
 

time: 58.3 us -> 58.1 us (level)
  no operation moved by 1% of the time
where the time goes in v6:
time: 58.1 us; the launch traced here: 57.8 us
  blocking collectives  18.2 us (31%)
  starting transfers between devices  12.4 us (21%)
  Pallas kernels  11.8 us (20%)
  waiting for transfers between devices  11.7 us (20%)
  local copies, waits for them, and re-layouts  3.6 us (6%)
    all_to_all x1, blocking collectives, per_device(): lax.all_to_all(timed, 'space', split_axis=0, concat_axis=1, tiled=True, a...  18.2 us
    all_to_all x1, waiting for transfers between devices, per_device(): lax.all_to_all(source, 'space', split_axis=1, concat_axis=0, tiled=True)  7.96 us
    all_to_all x1, starting transfers between devices, per_device(): lax.all_to_all(source, 'space', split_axis=1, concat_axis=0, tiled=True)  7.38 us
    ppermute x3, starting transfers between devices, swap(): lax.ppermute(outer, ('group', 'space'), outer_pairs)  4.53 us
    ppermute x3, waiting for transfers between devices, swap(): lax.ppermute(outer, ('group', 'space'), outer_pairs)  3.74 us
    unnamed x16, local copies, waits for them, and re-layouts  3.6 us
    pallas_call x1, Pallas kernels, per_device(): call(functools.partial(build_kernel, count), (*[bf16(SLOTS * BS, own)] *...  2.9 us
    pallas_call x1, Pallas kernels, per_device(): call(own_first_kernel, (value, ahead, *[bf16(side, own)] * 2, *[bf16(2 *...  2.65 us
  transfers between devices with their start and end apart: 7, of which 4 were waited for; matrix products, arithmetic and copies ran while one was open for 0% of the time, Pallas kernels for 16%

profile of v6, /device:TPU:0, one launch (start us, length us, event | category | flops | bytes accessed | tf_op | source)
XLA Modules:
  0.0 57.8 jit_solution(3490716050740518141)
XLA Ops:
  0.0 7.4 %all-to-all-start = ((f32[8,16,1024]{2,0,1:T(8,128)}), f32[8,16,1024]{2,0,1:T(8,128)S(1)}, u32[]{:S(2)}, u32[]{:S(2)}) async-start(f32[8,16,1024]{2,0,1:T(8,128)} %bitcast.16), calls=%async_computation | async-start | bytes 1048576 | tf_op jit(solution)/shard_map/all_to_all | solution.py:264
  7.4 0.0 copy-start
  7.4 1.6 %copy-done = f32[16,64,448]{2,1,0:T(8,128)S(1)} copy-done((f32[16,64,448]{2,1,0:T(8,128)S(1)}, f32[16,64,448]{2,1,0:T(8,128)}, u32[]{:S(2)}) %copy-start) | copy-done | bytes 1835032
  9.0 0.0 copy-start.5
  9.0 0.7 %copy-done.5 = s32[16,7]{0,1:T(8,128)S(1)} copy-done((s32[16,7]{0,1:T(8,128)S(1)}, s32[16,7]{0,1:T(8,128)}, u32[]{:S(2)}) %copy-start.5) | copy-done | bytes 472
  9.7 0.0 copy-start.6
  9.7 0.7 %copy-done.6 = s32[4]{0:T(128)S(1)} copy-done((s32[4]{0:T(128)S(1)}, s32[4]{0:T(128)}, u32[]{:S(2)}) %copy-start.6) | copy-done | bytes 40
  10.3 0.0 copy-start.7
  10.3 0.7 %copy-done.7 = s32[4]{0:T(128)S(1)} copy-done((s32[4]{0:T(128)S(1)}, s32[4]{0:T(128)}, u32[]{:S(2)}) %copy-start.7) | copy-done | bytes 40
  11.0 2.9 %operator.1 = (bf16[448,1024]{1,0:T(8,128)(2,1)S(1)}, bf16[448,1024]{1,0:T(8,128)(2,1)S(1)}, bf16[1024,512]{1,0:T(8,128)(2,1)S(1)}, s32[8,16]{1,0:T(8,128)S(1)}) custom-call(s32[1]{0:T(128)} %bitcast.4.me_ref, s32[7,16]{1,0:T(8,128)S(1)} %bitcast.15, s32[4]{0:T(128)S(1)} %copy-done.6, s32[4]{0:T(128)S(1)} %copy-done.7, f32[16,64,448]{2,1,0:T(8,128)S(1)} %copy-done), custom_call_target="tpu_custom_call" | custom-call | flops 268435456 | bytes 16777216 | tf_op jit(solution)/shard_map/operator/pallas_call | solution.py:267
  13.9 8.0 %all-to-all-done = f32[8,16,1024]{2,0,1:T(8,128)S(1)} async-done(((f32[8,16,1024]{2,0,1:T(8,128)}), f32[8,16,1024]{2,0,1:T(8,128)S(1)}, u32[]{:S(2)}, u32[]{:S(2)}) %all-to-all-start) | async-done | bytes 524320 | tf_op jit(solution)/shard_map/all_to_all | solution.py:264
  21.9 0.0 copy-start.3
  21.9 0.0 copy-start.4
  21.9 0.4 send_0.1
  22.3 0.1 collective-permute-start
  22.4 1.6 %collective-permute-start.1 = (f32[128,256]{1,0:T(8,128)S(1)}, f32[128,256]{1,0:T(8,128)S(1)}, u32[]{:S(2)}, u32[]{:S(2)}) collective-permute-start(f32[128,256]{1,0:T(8,128)S(1)} %get-tuple-element.30), channel_id=1, source_target_pairs={{1,2},{2,1},{3,4},{4,3},{5,6},{6,5},{7,8},{8,7},{9,10},{10,9},{11,... | collective-permute-start | bytes 393224 | tf_op jit(solution)/shard_map/ppermute | solution.py:262
  23.9 2.6 %own_1.1 = (f32[128,1024]{1,0:T(8,128)S(1)}, f32[128,512]{1,0:T(8,128)S(1)}, bf16[1536,1024]{1,0:T(8,128)(2,1)S(1)}, bf16[1536,1024]{1,0:T(8,128)(2,1)S(1)}, bf1...) custom-call(f32[128,1024]{1,0:T(8,128)S(1)} %bitcast.11, bf16[448,1024]{1,0:T(8,128)(2,1)S(1)} %get-tuple-element.24.blocks_high, ...), custom_call_target="tpu_custom_call" | custom-call | flops 268435456 | bytes 4194304 | tf_op jit(solution)/shard_map/own_1/pallas_call | solution.py:285
  26.6 0.0 collective-permute-done.from_inner
  26.6 0.8 %collective-permute-done.1.from_outer = f32[128,256]{1,0:T(8,128)S(1)} collective-permute-done((f32[128,256]{1,0:T(8,128)S(1)}, f32[128,256]{1,0:T(8,128)S(1)}, u32[]{:S(2)}, u32[]{:S(2)}) %collective-permute-start.1) | collective-permute-done | bytes 131104 | tf_op jit(solution)/shard_map/ppermute | solution.py:262
  27.4 0.4 send_1.1
  27.8 0.2 collective-permute-start.2
  28.0 1.5 %collective-permute-start.3 = (f32[128,256]{1,0:T(8,128)S(1)}, f32[128,256]{1,0:T(8,128)S(1)}, u32[]{:S(2)}, u32[]{:S(2)}) collective-permute-start(f32[128,256]{1,0:T(8,128)S(1)} %get-tuple-element.38), channel_id=1, source_target_pairs={{1,2},{2,1},{3,4},{4,3},{5,6},{6,5},{7,8},{8,7},{9,10},{10,9},{11,... | collective-permute-start | bytes 393224 | tf_op jit(solution)/shard_map/ppermute | solution.py:262
  29.5 0.0 copy-done.3
  29.5 0.0 copy-done.4
  29.5 0.0 copy-start.1
  29.5 0.0 copy-start.2
  29.5 2.1 %own_2.1 = (f32[128,1024]{1,0:T(8,128)S(1)}, f32[128,512]{1,0:T(8,128)S(1)}, f32[128,1024]{1,0:T(8,128)S(1)}) custom-call(f32[128,1024]{1,0:T(8,128)S(1)} %bitcast.12, f32[128,1024]{1,0:T(8,128)S(1)} %get-tuple-element.28.part_ref, f32[128,256]{1,0:T(8,128)S(1)} %collective-permute-done.from_inner, f32[128,256]{1,0:T(8,128)S(1)} %collective-permute-done.1.from_outer, ...), custom_call_target="tpu_custom_call" | custom-call | flops 268435456 | bytes 4194304 | tf_op jit(solution)/shard_map/own_2/pallas_call | solution.py:294
  31.6 0.0 collective-permute-done.2.from_inner
  31.6 1.3 %collective-permute-done.3.from_outer = f32[128,256]{1,0:T(8,128)S(1)} collective-permute-done((f32[128,256]{1,0:T(8,128)S(1)}, f32[128,256]{1,0:T(8,128)S(1)}, u32[]{:S(2)}, u32[]{:S(2)}) %collective-permute-start.3) | collective-permute-done | bytes 131104 | tf_op jit(solution)/shard_map/ppermute | solution.py:262
  32.9 0.0 copy-done.1
  32.9 0.4 send_2.1
  33.3 0.2 collective-permute-start.4
  33.5 1.5 %collective-permute-start.5 = (f32[128,256]{1,0:T(8,128)S(1)}, f32[128,256]{1,0:T(8,128)S(1)}, u32[]{:S(2)}, u32[]{:S(2)}) collective-permute-start(f32[128,256]{1,0:T(8,128)S(1)} %get-tuple-element.42), channel_id=1, source_target_pairs={{1,2},{2,1},{3,4},{4,3},{5,6},{6,5},{7,8},{8,7},{9,10},{10,9},{11,... | collective-permute-start | bytes 393224 | tf_op jit(solution)/shard_map/ppermute | solution.py:262
  35.0 0.0 copy-done.2
  35.0 1.9 %own_3.1.part_ref = f32[128,1024]{1,0:T(8,128)S(1)} custom-call(f32[128,1024]{1,0:T(8,128)S(1)} %get-tuple-element.33.part_ref, f32[128,256]{1,0:T(8,128)S(1)} %collective-permute-done.2.from_inner, f32[128,256]{1,0:T(8,128)S(1)} %collective-permute-done.3.from_outer, f32[128,1024]{1,0:T(8,128)S(1)} %get-tuple-element.39.total_ref, ...), custom_call_target="tpu_custom_call" | custom-call | flops 268435456 | bytes 4194304 | tf_op jit(solution)/shard_map/own_3/pallas_call | solution.py:302
  36.9 0.0 collective-permute-done.4.from_inner
  36.9 1.6 %collective-permute-done.5.from_outer = f32[128,256]{1,0:T(8,128)S(1)} collective-permute-done((f32[128,256]{1,0:T(8,128)S(1)}, f32[128,256]{1,0:T(8,128)S(1)}, u32[]{:S(2)}, u32[]{:S(2)}) %collective-permute-start.5) | collective-permute-done | bytes 131104 | tf_op jit(solution)/shard_map/ppermute | solution.py:262
  38.5 0.3 close.1
  38.8 18.2 %all_to_all.38 = f32[16,8,1024]{2,1,0:T(8,128)S(1)} all-to-all(f32[16,8,1024]{2,1,0:T(8,128)S(1)} %bitcast.13), channel_id=1, replica_groups={{5,8,12,4,9,10,6,7,14,1,15,2,11,13,3,0},{21,24,28,20,25,26,22,23,30,17,..., dimensions={0} | all-to-all | bytes 1048576 | tf_op jit(solution)/shard_map/all_to_all | solution.py:304
  57.0 0.8 %store.1 = f32[8,16384]{1,0:T(8,128)} custom-call(f32[8,16384]{1,0:T(8,128)S(1)} %bitcast.14), custom_call_target="tpu_custom_call" | custom-call | flops 268435456 | bytes 4194304 | tf_op jit(solution)/shard_map/store/pallas_call | solution.py:307
Async XLA Ops:
  0.0 21.9 %all-to-all-start = ((f32[8,16,1024]{2,0,1:T(8,128)}), f32[8,16,1024]{2,0,1:T(8,128)S(1)}, u32[]{:S(2)}, u32[]{:S(2)}) async-start(f32[8,16,1024]{2,0,1:T(8,128)} %bitcast.16), calls=%async_computation | async-start | bytes 1048576 | tf_op jit(solution)/shard_map/all_to_all | solution.py:264
  7.4 1.6 %copy-start = (f32[16,64,448]{2,1,0:T(8,128)S(1)}, f32[16,64,448]{2,1,0:T(8,128)}, u32[]{:S(2)}) copy-start(f32[16,64,448]{2,1,0:T(8,128)} %blocks_in.1) | copy-start | bytes 5505028
  9.0 0.7 %copy-start.5 = (s32[16,7]{0,1:T(8,128)S(1)}, s32[16,7]{0,1:T(8,128)}, u32[]{:S(2)}) copy-start(s32[16,7]{0,1:T(8,128)} %param.11) | copy-start | bytes 1348
  9.7 0.7 %copy-start.6 = (s32[4]{0:T(128)S(1)}, s32[4]{0:T(128)}, u32[]{:S(2)}) copy-start(s32[4]{0:T(128)} %up_ref.1) | copy-start | bytes 52
  10.3 0.7 %copy-start.7 = (s32[4]{0:T(128)S(1)}, s32[4]{0:T(128)}, u32[]{:S(2)}) copy-start(s32[4]{0:T(128)} %down_ref.1) | copy-start | bytes 52
  21.9 7.6 %copy-start.3 = (bf16[256,128]{1,0:T(8,128)(2,1)S(1)}, bf16[256,128]{1,0:T(8,128)(2,1)}, u32[]{:S(2)}) copy-start(bf16[256,128]{1,0:T(8,128)(2,1)} %constant.25.table0_ref) | copy-start | bytes 196612
  21.9 7.6 %copy-start.4 = (bf16[256,128]{1,0:T(8,128)(2,1)S(1)}, bf16[256,128]{1,0:T(8,128)(2,1)}, u32[]{:S(2)}) copy-start(bf16[256,128]{1,0:T(8,128)(2,1)} %constant.30.table1_ref) | copy-start | bytes 196612
  22.3 4.3 %collective-permute-start = (f32[128,256]{1,0:T(8,128)S(1)}, f32[128,256]{1,0:T(8,128)S(1)}, u32[]{:S(2)}, u32[]{:S(2)}) collective-permute-start(f32[128,256]{1,0:T(8,128)S(1)} %get-tuple-element.29), channel_id=1, source_target_pairs={{0,1},{1,0},{2,3},{3,2},{4,5},{5,4},{6,7},{7,6},{8,9},{9,8},{10,11... | collective-permute-start | bytes 393224 | tf_op jit(solution)/shard_map/ppermute | solution.py:262
  22.4 5.0 %collective-permute-start.1 = (f32[128,256]{1,0:T(8,128)S(1)}, f32[128,256]{1,0:T(8,128)S(1)}, u32[]{:S(2)}, u32[]{:S(2)}) collective-permute-start(f32[128,256]{1,0:T(8,128)S(1)} %get-tuple-element.30), channel_id=1, source_target_pairs={{1,2},{2,1},{3,4},{4,3},{5,6},{6,5},{7,8},{8,7},{9,10},{10,9},{11,... | collective-permute-start | bytes 393224 | tf_op jit(solution)/shard_map/ppermute | solution.py:262
  27.8 3.8 %collective-permute-start.2 = (f32[128,256]{1,0:T(8,128)S(1)}, f32[128,256]{1,0:T(8,128)S(1)}, u32[]{:S(2)}, u32[]{:S(2)}) collective-permute-start(f32[128,256]{1,0:T(8,128)S(1)} %get-tuple-element.37), channel_id=1, source_target_pairs={{0,1},{1,0},{2,3},{3,2},{4,5},{5,4},{6,7},{7,6},{8,9},{9,8},{10,11... | collective-permute-start | bytes 393224 | tf_op jit(solution)/shard_map/ppermute | solution.py:262
  28.0 5.0 %collective-permute-start.3 = (f32[128,256]{1,0:T(8,128)S(1)}, f32[128,256]{1,0:T(8,128)S(1)}, u32[]{:S(2)}, u32[]{:S(2)}) collective-permute-start(f32[128,256]{1,0:T(8,128)S(1)} %get-tuple-element.38), channel_id=1, source_target_pairs={{1,2},{2,1},{3,4},{4,3},{5,6},{6,5},{7,8},{8,7},{9,10},{10,9},{11,... | collective-permute-start | bytes 393224 | tf_op jit(solution)/shard_map/ppermute | solution.py:262
  29.5 3.5 %copy-start.1 = (bf16[256,128]{1,0:T(8,128)(2,1)S(1)}, bf16[256,128]{1,0:T(8,128)(2,1)}, u32[]{:S(2)}) copy-start(bf16[256,128]{1,0:T(8,128)(2,1)} %constant.40.table3_ref.table_ref) | copy-start | bytes 196612
  29.5 5.5 %copy-start.2 = (bf16[256,128]{1,0:T(8,128)(2,1)S(1)}, bf16[256,128]{1,0:T(8,128)(2,1)}, u32[]{:S(2)}) copy-start(bf16[256,128]{1,0:T(8,128)(2,1)} %constant.35.table2_ref) | copy-start | bytes 196612
  33.3 3.5 %collective-permute-start.4 = (f32[128,256]{1,0:T(8,128)S(1)}, f32[128,256]{1,0:T(8,128)S(1)}, u32[]{:S(2)}, u32[]{:S(2)}) collective-permute-start(f32[128,256]{1,0:T(8,128)S(1)} %get-tuple-element.41), channel_id=1, source_target_pairs={{0,1},{1,0},{2,3},{3,2},{4,5},{5,4},{6,7},{7,6},{8,9},{9,8},{10,11... | collective-permute-start | bytes 393224 | tf_op jit(solution)/shard_map/ppermute | solution.py:262
  33.5 5.0 %collective-permute-start.5 = (f32[128,256]{1,0:T(8,128)S(1)}, f32[128,256]{1,0:T(8,128)S(1)}, u32[]{:S(2)}, u32[]{:S(2)}) collective-permute-start(f32[128,256]{1,0:T(8,128)S(1)} %get-tuple-element.42), channel_id=1, source_target_pairs={{1,2},{2,1},{3,4},{4,3},{5,6},{6,5},{7,8},{8,7},{9,10},{10,9},{11,... | collective-permute-start | bytes 393224 | tf_op jit(solution)/shard_map/ppermute | solution.py:262

commit v7 on v6

--- a/solution.py
+++ b/solution.py
@@ -13,7 +13,7 @@
 SHIFT_SCALE = 2.0
 DIAG_CENTER = 4.0
 TERMS = 4
-SEND_ORDER = (5, 8, 12, 4, 9, 10, 6, 7, 14, 1, 15, 2, 11, 13, 3, 0)
+SEND_ORDER = (9, 13, 5, 1, 12, 0, 15, 10, 4, 7, 14, 3, 6, 2, 11, 8)
 VMEM = pl.BlockSpec(memory_space=pltpu.VMEM)
 SMEM = pl.BlockSpec(memory_space=pltpu.SMEM)
 ANY = pl.BlockSpec(memory_space=pl.ANY)

time: 58.1 us -> 58.2 us (level)
  transfers between devices with their start and end apart: 7 -> 7, of which waited for: 4 -> 4; matrix products, arithmetic and copies ran while one was open for 0% -> 0% of each run, Pallas kernels for 16% -> 17%
where the time goes in v7:
time: 58.2 us; the launch traced here: 57.4 us
  blocking collectives  17.9 us (31%)
  starting transfers between devices  12.4 us (21%)
  Pallas kernels  11.8 us (20%)
  waiting for transfers between devices  11.7 us (20%)
  local copies, waits for them, and re-layouts  3.6 us (6%)
    all_to_all x1, blocking collectives, per_device(): lax.all_to_all(timed, 'space', split_axis=0, concat_axis=1, tiled=True, a...  17.9 us
    all_to_all x1, waiting for transfers between devices, per_device(): lax.all_to_all(source, 'space', split_axis=1, concat_axis=0, tiled=True)  7.96 us
    all_to_all x1, starting transfers between devices, per_device(): lax.all_to_all(source, 'space', split_axis=1, concat_axis=0, tiled=True)  7.38 us
    ppermute x3, starting transfers between devices, swap(): lax.ppermute(outer, ('group', 'space'), outer_pairs)  4.53 us
    ppermute x3, waiting for transfers between devices, swap(): lax.ppermute(outer, ('group', 'space'), outer_pairs)  3.75 us
    unnamed x16, local copies, waits for them, and re-layouts  3.6 us
    pallas_call x1, Pallas kernels, per_device(): call(functools.partial(build_kernel, count), (*[bf16(SLOTS * BS, own)] *...  2.9 us
    pallas_call x1, Pallas kernels, per_device(): call(own_first_kernel, (value, ahead, *[bf16(side, own)] * 2, *[bf16(2 *...  2.65 us
  transfers between devices with their start and end apart: 7, of which 4 were waited for; matrix products, arithmetic and copies ran while one was open for 0% of the time, Pallas kernels for 17%

profile of v7, /device:TPU:0, one launch (start us, length us, event | category | flops | bytes accessed | tf_op | source)
XLA Modules:
  0.0 57.4 jit_solution(16082475338790588093)
XLA Ops:
  0.0 7.4 %all-to-all-start = ((f32[8,16,1024]{2,0,1:T(8,128)}), f32[8,16,1024]{2,0,1:T(8,128)S(1)}, u32[]{:S(2)}, u32[]{:S(2)}) async-start(f32[8,16,1024]{2,0,1:T(8,128)} %bitcast.16), calls=%async_computation | async-start | bytes 1048576 | tf_op jit(solution)/shard_map/all_to_all | solution.py:264
  7.4 0.0 copy-start
  7.4 1.6 %copy-done = f32[16,64,448]{2,1,0:T(8,128)S(1)} copy-done((f32[16,64,448]{2,1,0:T(8,128)S(1)}, f32[16,64,448]{2,1,0:T(8,128)}, u32[]{:S(2)}) %copy-start) | copy-done | bytes 1835032
  9.0 0.0 copy-start.5
  9.0 0.7 %copy-done.5 = s32[16,7]{0,1:T(8,128)S(1)} copy-done((s32[16,7]{0,1:T(8,128)S(1)}, s32[16,7]{0,1:T(8,128)}, u32[]{:S(2)}) %copy-start.5) | copy-done | bytes 472
  9.7 0.0 copy-start.6
  9.7 0.7 %copy-done.6 = s32[4]{0:T(128)S(1)} copy-done((s32[4]{0:T(128)S(1)}, s32[4]{0:T(128)}, u32[]{:S(2)}) %copy-start.6) | copy-done | bytes 40
  10.3 0.0 copy-start.7
  10.3 0.7 %copy-done.7 = s32[4]{0:T(128)S(1)} copy-done((s32[4]{0:T(128)S(1)}, s32[4]{0:T(128)}, u32[]{:S(2)}) %copy-start.7) | copy-done | bytes 40
  11.0 2.9 %operator.1 = (bf16[448,1024]{1,0:T(8,128)(2,1)S(1)}, bf16[448,1024]{1,0:T(8,128)(2,1)S(1)}, bf16[1024,512]{1,0:T(8,128)(2,1)S(1)}, s32[8,16]{1,0:T(8,128)S(1)}) custom-call(s32[1]{0:T(128)} %bitcast.4.me_ref, s32[7,16]{1,0:T(8,128)S(1)} %bitcast.15, s32[4]{0:T(128)S(1)} %copy-done.6, s32[4]{0:T(128)S(1)} %copy-done.7, f32[16,64,448]{2,1,0:T(8,128)S(1)} %copy-done), custom_call_target="tpu_custom_call" | custom-call | flops 268435456 | bytes 16777216 | tf_op jit(solution)/shard_map/operator/pallas_call | solution.py:267
  13.9 8.0 %all-to-all-done = f32[8,16,1024]{2,0,1:T(8,128)S(1)} async-done(((f32[8,16,1024]{2,0,1:T(8,128)}), f32[8,16,1024]{2,0,1:T(8,128)S(1)}, u32[]{:S(2)}, u32[]{:S(2)}) %all-to-all-start) | async-done | bytes 524320 | tf_op jit(solution)/shard_map/all_to_all | solution.py:264
  21.9 0.0 copy-start.3
  21.9 0.0 copy-start.4
  21.9 0.4 send_0.1
  22.3 0.1 collective-permute-start
  22.4 1.6 %collective-permute-start.1 = (f32[128,256]{1,0:T(8,128)S(1)}, f32[128,256]{1,0:T(8,128)S(1)}, u32[]{:S(2)}, u32[]{:S(2)}) collective-permute-start(f32[128,256]{1,0:T(8,128)S(1)} %get-tuple-element.30), channel_id=1, source_target_pairs={{1,2},{2,1},{3,4},{4,3},{5,6},{6,5},{7,8},{8,7},{9,10},{10,9},{11,... | collective-permute-start | bytes 393224 | tf_op jit(solution)/shard_map/ppermute | solution.py:262
  23.9 2.6 %own_1.1 = (f32[128,1024]{1,0:T(8,128)S(1)}, f32[128,512]{1,0:T(8,128)S(1)}, bf16[1536,1024]{1,0:T(8,128)(2,1)S(1)}, bf16[1536,1024]{1,0:T(8,128)(2,1)S(1)}, bf1...) custom-call(f32[128,1024]{1,0:T(8,128)S(1)} %bitcast.11, bf16[448,1024]{1,0:T(8,128)(2,1)S(1)} %get-tuple-element.24.blocks_high, ...), custom_call_target="tpu_custom_call" | custom-call | flops 268435456 | bytes 4194304 | tf_op jit(solution)/shard_map/own_1/pallas_call | solution.py:285
  26.6 0.0 collective-permute-done.from_inner
  26.6 0.8 %collective-permute-done.1.from_outer = f32[128,256]{1,0:T(8,128)S(1)} collective-permute-done((f32[128,256]{1,0:T(8,128)S(1)}, f32[128,256]{1,0:T(8,128)S(1)}, u32[]{:S(2)}, u32[]{:S(2)}) %collective-permute-start.1) | collective-permute-done | bytes 131104 | tf_op jit(solution)/shard_map/ppermute | solution.py:262
  27.4 0.4 send_1.1
  27.8 0.2 collective-permute-start.2
  28.0 1.5 %collective-permute-start.3 = (f32[128,256]{1,0:T(8,128)S(1)}, f32[128,256]{1,0:T(8,128)S(1)}, u32[]{:S(2)}, u32[]{:S(2)}) collective-permute-start(f32[128,256]{1,0:T(8,128)S(1)} %get-tuple-element.38), channel_id=1, source_target_pairs={{1,2},{2,1},{3,4},{4,3},{5,6},{6,5},{7,8},{8,7},{9,10},{10,9},{11,... | collective-permute-start | bytes 393224 | tf_op jit(solution)/shard_map/ppermute | solution.py:262
  29.5 0.0 copy-done.3
  29.5 0.0 copy-done.4
  29.5 0.0 copy-start.1
  29.5 0.0 copy-start.2
  29.5 2.1 %own_2.1 = (f32[128,1024]{1,0:T(8,128)S(1)}, f32[128,512]{1,0:T(8,128)S(1)}, f32[128,1024]{1,0:T(8,128)S(1)}) custom-call(f32[128,1024]{1,0:T(8,128)S(1)} %bitcast.12, f32[128,1024]{1,0:T(8,128)S(1)} %get-tuple-element.28.part_ref, f32[128,256]{1,0:T(8,128)S(1)} %collective-permute-done.from_inner, f32[128,256]{1,0:T(8,128)S(1)} %collective-permute-done.1.from_outer, ...), custom_call_target="tpu_custom_call" | custom-call | flops 268435456 | bytes 4194304 | tf_op jit(solution)/shard_map/own_2/pallas_call | solution.py:294
  31.6 0.0 collective-permute-done.2.from_inner
  31.6 1.3 %collective-permute-done.3.from_outer = f32[128,256]{1,0:T(8,128)S(1)} collective-permute-done((f32[128,256]{1,0:T(8,128)S(1)}, f32[128,256]{1,0:T(8,128)S(1)}, u32[]{:S(2)}, u32[]{:S(2)}) %collective-permute-start.3) | collective-permute-done | bytes 131104 | tf_op jit(solution)/shard_map/ppermute | solution.py:262
  32.9 0.0 copy-done.1
  32.9 0.4 send_2.1
  33.3 0.2 collective-permute-start.4
  33.5 1.5 %collective-permute-start.5 = (f32[128,256]{1,0:T(8,128)S(1)}, f32[128,256]{1,0:T(8,128)S(1)}, u32[]{:S(2)}, u32[]{:S(2)}) collective-permute-start(f32[128,256]{1,0:T(8,128)S(1)} %get-tuple-element.42), channel_id=1, source_target_pairs={{1,2},{2,1},{3,4},{4,3},{5,6},{6,5},{7,8},{8,7},{9,10},{10,9},{11,... | collective-permute-start | bytes 393224 | tf_op jit(solution)/shard_map/ppermute | solution.py:262
  35.0 0.0 copy-done.2
  35.0 1.9 %own_3.1.part_ref = f32[128,1024]{1,0:T(8,128)S(1)} custom-call(f32[128,1024]{1,0:T(8,128)S(1)} %get-tuple-element.33.part_ref, f32[128,256]{1,0:T(8,128)S(1)} %collective-permute-done.2.from_inner, f32[128,256]{1,0:T(8,128)S(1)} %collective-permute-done.3.from_outer, f32[128,1024]{1,0:T(8,128)S(1)} %get-tuple-element.39.total_ref, ...), custom_call_target="tpu_custom_call" | custom-call | flops 268435456 | bytes 4194304 | tf_op jit(solution)/shard_map/own_3/pallas_call | solution.py:302
  36.9 0.0 collective-permute-done.4.from_inner
  36.9 1.6 %collective-permute-done.5.from_outer = f32[128,256]{1,0:T(8,128)S(1)} collective-permute-done((f32[128,256]{1,0:T(8,128)S(1)}, f32[128,256]{1,0:T(8,128)S(1)}, u32[]{:S(2)}, u32[]{:S(2)}) %collective-permute-start.5) | collective-permute-done | bytes 131104 | tf_op jit(solution)/shard_map/ppermute | solution.py:262
  38.5 0.3 close.1
  38.8 17.9 %all_to_all.38 = f32[16,8,1024]{2,1,0:T(8,128)S(1)} all-to-all(f32[16,8,1024]{2,1,0:T(8,128)S(1)} %bitcast.13), channel_id=1, replica_groups={{9,13,5,1,12,0,15,10,4,7,14,3,6,2,11,8},{25,29,21,17,28,16,31,26,20,23,..., dimensions={0} | all-to-all | bytes 1048576 | tf_op jit(solution)/shard_map/all_to_all | solution.py:304
  56.7 0.8 %store.1 = f32[8,16384]{1,0:T(8,128)} custom-call(f32[8,16384]{1,0:T(8,128)S(1)} %bitcast.14), custom_call_target="tpu_custom_call" | custom-call | flops 268435456 | bytes 4194304 | tf_op jit(solution)/shard_map/store/pallas_call | solution.py:307
Async XLA Ops:
  0.0 21.9 %all-to-all-start = ((f32[8,16,1024]{2,0,1:T(8,128)}), f32[8,16,1024]{2,0,1:T(8,128)S(1)}, u32[]{:S(2)}, u32[]{:S(2)}) async-start(f32[8,16,1024]{2,0,1:T(8,128)} %bitcast.16), calls=%async_computation | async-start | bytes 1048576 | tf_op jit(solution)/shard_map/all_to_all | solution.py:264
  7.4 1.6 %copy-start = (f32[16,64,448]{2,1,0:T(8,128)S(1)}, f32[16,64,448]{2,1,0:T(8,128)}, u32[]{:S(2)}) copy-start(f32[16,64,448]{2,1,0:T(8,128)} %blocks_in.1) | copy-start | bytes 5505028
  9.0 0.7 %copy-start.5 = (s32[16,7]{0,1:T(8,128)S(1)}, s32[16,7]{0,1:T(8,128)}, u32[]{:S(2)}) copy-start(s32[16,7]{0,1:T(8,128)} %param.11) | copy-start | bytes 1348
  9.7 0.7 %copy-start.6 = (s32[4]{0:T(128)S(1)}, s32[4]{0:T(128)}, u32[]{:S(2)}) copy-start(s32[4]{0:T(128)} %up_ref.1) | copy-start | bytes 52
  10.3 0.7 %copy-start.7 = (s32[4]{0:T(128)S(1)}, s32[4]{0:T(128)}, u32[]{:S(2)}) copy-start(s32[4]{0:T(128)} %down_ref.1) | copy-start | bytes 52
  21.9 7.6 %copy-start.3 = (bf16[256,128]{1,0:T(8,128)(2,1)S(1)}, bf16[256,128]{1,0:T(8,128)(2,1)}, u32[]{:S(2)}) copy-start(bf16[256,128]{1,0:T(8,128)(2,1)} %constant.25.table0_ref) | copy-start | bytes 196612
  21.9 7.6 %copy-start.4 = (bf16[256,128]{1,0:T(8,128)(2,1)S(1)}, bf16[256,128]{1,0:T(8,128)(2,1)}, u32[]{:S(2)}) copy-start(bf16[256,128]{1,0:T(8,128)(2,1)} %constant.30.table1_ref) | copy-start | bytes 196612
  22.3 4.3 %collective-permute-start = (f32[128,256]{1,0:T(8,128)S(1)}, f32[128,256]{1,0:T(8,128)S(1)}, u32[]{:S(2)}, u32[]{:S(2)}) collective-permute-start(f32[128,256]{1,0:T(8,128)S(1)} %get-tuple-element.29), channel_id=1, source_target_pairs={{0,1},{1,0},{2,3},{3,2},{4,5},{5,4},{6,7},{7,6},{8,9},{9,8},{10,11... | collective-permute-start | bytes 393224 | tf_op jit(solution)/shard_map/ppermute | solution.py:262
  22.4 5.0 %collective-permute-start.1 = (f32[128,256]{1,0:T(8,128)S(1)}, f32[128,256]{1,0:T(8,128)S(1)}, u32[]{:S(2)}, u32[]{:S(2)}) collective-permute-start(f32[128,256]{1,0:T(8,128)S(1)} %get-tuple-element.30), channel_id=1, source_target_pairs={{1,2},{2,1},{3,4},{4,3},{5,6},{6,5},{7,8},{8,7},{9,10},{10,9},{11,... | collective-permute-start | bytes 393224 | tf_op jit(solution)/shard_map/ppermute | solution.py:262
  27.8 3.8 %collective-permute-start.2 = (f32[128,256]{1,0:T(8,128)S(1)}, f32[128,256]{1,0:T(8,128)S(1)}, u32[]{:S(2)}, u32[]{:S(2)}) collective-permute-start(f32[128,256]{1,0:T(8,128)S(1)} %get-tuple-element.37), channel_id=1, source_target_pairs={{0,1},{1,0},{2,3},{3,2},{4,5},{5,4},{6,7},{7,6},{8,9},{9,8},{10,11... | collective-permute-start | bytes 393224 | tf_op jit(solution)/shard_map/ppermute | solution.py:262
  28.0 5.0 %collective-permute-start.3 = (f32[128,256]{1,0:T(8,128)S(1)}, f32[128,256]{1,0:T(8,128)S(1)}, u32[]{:S(2)}, u32[]{:S(2)}) collective-permute-start(f32[128,256]{1,0:T(8,128)S(1)} %get-tuple-element.38), channel_id=1, source_target_pairs={{1,2},{2,1},{3,4},{4,3},{5,6},{6,5},{7,8},{8,7},{9,10},{10,9},{11,... | collective-permute-start | bytes 393224 | tf_op jit(solution)/shard_map/ppermute | solution.py:262
  29.5 3.5 %copy-start.1 = (bf16[256,128]{1,0:T(8,128)(2,1)S(1)}, bf16[256,128]{1,0:T(8,128)(2,1)}, u32[]{:S(2)}) copy-start(bf16[256,128]{1,0:T(8,128)(2,1)} %constant.40.table3_ref.table_ref) | copy-start | bytes 196612
  29.5 5.5 %copy-start.2 = (bf16[256,128]{1,0:T(8,128)(2,1)S(1)}, bf16[256,128]{1,0:T(8,128)(2,1)}, u32[]{:S(2)}) copy-start(bf16[256,128]{1,0:T(8,128)(2,1)} %constant.35.table2_ref) | copy-start | bytes 196612
  33.3 3.5 %collective-permute-start.4 = (f32[128,256]{1,0:T(8,128)S(1)}, f32[128,256]{1,0:T(8,128)S(1)}, u32[]{:S(2)}, u32[]{:S(2)}) collective-permute-start(f32[128,256]{1,0:T(8,128)S(1)} %get-tuple-element.41), channel_id=1, source_target_pairs={{0,1},{1,0},{2,3},{3,2},{4,5},{5,4},{6,7},{7,6},{8,9},{9,8},{10,11... | collective-permute-start | bytes 393224 | tf_op jit(solution)/shard_map/ppermute | solution.py:262
  33.5 5.0 %collective-permute-start.5 = (f32[128,256]{1,0:T(8,128)S(1)}, f32[128,256]{1,0:T(8,128)S(1)}, u32[]{:S(2)}, u32[]{:S(2)}) collective-permute-start(f32[128,256]{1,0:T(8,128)S(1)} %get-tuple-element.42), channel_id=1, source_target_pairs={{1,2},{2,1},{3,4},{4,3},{5,6},{6,5},{7,8},{8,7},{9,10},{10,9},{11,... | collective-permute-start | bytes 393224 | tf_op jit(solution)/shard_map/ppermute | solution.py:262
